TPU v7x, 768 devices: a whole 4x8x12 slice. The times are simulated.
768 devices in a mesh: lat: 96 (over x, z, core), lon: 8 (over y).
Axes of the slice: x: 4, y: 8, z: 12, core: 2. Of those that a mesh axis runs over, the one named last changes fastest.
Arguments:
- wind_u: float32 [8, 1536, 2560], P(None, 'lat', 'lon'), may hold values from -6 to 6
- wind_v: float32 [8, 1536, 2560], P(None, 'lat', 'lon'), may hold values from -6 to 6
- basis: bfloat16 [864, 640, 768], P('lat'), may hold values from -6 to 6
- wave_slots: int32 [640], replicated, may hold values from 0 to 863, as said below
- degree_count: int32 [640], replicated, may hold values from 1 to 640, as said below
- viscosity: float32 [8], replicated, may hold values from 0.5 to 50
Outputs:
- spectral: float32 [864, 8, 2, 2, 640], P('lat', 'lon')
- tendency: float32 [8, 2, 1536, 2560], P(None, None, 'lat', 'lon')
Inputs may be any that keep to these rules, and one draw needn't show every extreme that they name: `wave_slots`: all values differ; slot s belongs to owner s // 9, so an owner holds at most 9 wavenumbers, and one owner holds exactly 9. degree_count[0] = 640, and degree_count[m] <= 640 - m.
All inputs are finite; a program needn't handle non-finite values.
Results may differ from a plain program's by a relative error of at most 0.0048.
Values may be sent and summed in bfloat16 or wider, within the bound.
A program may use at most 128 MiB of HBM per device.

v0:
```python
import math

import jax
import jax.numpy as jnp
from jax import lax
from jax.sharding import PartitionSpec as P


def wave_table(col_count, full_length, waves):
    columns = jnp.arange(col_count, dtype=jnp.int32)
    wave_ids = jnp.arange(waves, dtype=jnp.int32)
    phases = columns[:, None] * wave_ids[None, :] % full_length
    angles = phases.astype(jnp.float32) * (2.0 * math.pi / full_length)
    scaling = 1.0 / math.sqrt(full_length)
    stacked = jnp.stack([jnp.cos(angles) * scaling, -jnp.sin(angles) * scaling], axis=2)
    return stacked.reshape(col_count, 2 * waves)


def to_slots(wave_rows, wave_of_slot, in_use):
    taken = jnp.take(wave_rows, wave_of_slot, axis=3)
    placed = jnp.where(in_use[:, None], taken, jnp.float32(0.0))
    shape = wave_rows.shape
    return placed.reshape(shape[0], shape[1], shape[2], 2 * wave_of_slot.shape[0])


def from_slots(slot_rows, wave_slots, table):
    shape = slot_rows.shape
    waves = wave_slots.shape[0]
    by_slot = slot_rows.reshape(shape[0], shape[1], shape[2], shape[3] // 2, 2)
    by_wave = jnp.take(by_slot, wave_slots, axis=3).astype(jnp.float32)
    weights = jnp.where(jnp.arange(waves, dtype=jnp.int32) == 0, 1.0, 2.0).astype(jnp.float32)
    weighted = (by_wave * weights[:, None]).reshape(-1, 2 * waves)
    grid_rows = lax.dot_general(
        weighted,
        table,
        (((1,), (1,)), ((), ())),
        precision=lax.Precision.HIGHEST,
        preferred_element_type=jnp.float32,
    )
    return grid_rows.reshape(shape[0], shape[1], shape[2], table.shape[0])


def body(wind_u, wind_v, basis, wave_slots, degree_count, viscosity):
    sectors = lax.axis_size("lon")
    sector_index = lax.axis_index("lon")
    owner_index = lax.axis_index("lat")
    levels, lat_rows, lon_cols = wind_u.shape
    level_dev = levels // sectors
    full_length = lon_cols * sectors
    capacity, degrees, half_lat = basis.shape
    latitudes = 2 * half_lat
    waves = wave_slots.shape[0]
    slot_total = capacity * lax.axis_size("lat")
    products = jnp.stack([wind_u * wind_v, wind_u * wind_u - wind_v * wind_v], axis=1)
    slot_ids = jnp.arange(slot_total, dtype=jnp.int32)
    matches = wave_slots[:, None] == slot_ids[None, :]
    wave_ids = jnp.arange(waves, dtype=jnp.int32)
    wave_of_slot = jnp.sum(jnp.where(matches, wave_ids[:, None], 0), axis=0)
    count_of_slot = jnp.sum(jnp.where(matches, degree_count[:, None], 0), axis=0)
    in_use = jnp.any(matches, axis=0)
    lon_lines = lax.all_to_all(products, "lon", split_axis=0, concat_axis=3, tiled=True)
    table = wave_table(full_length, full_length, waves)
    wave_rows = jnp.dot(
        lon_lines.reshape(-1, full_length),
        table,
        precision=lax.Precision.HIGHEST,
        preferred_element_type=jnp.float32,
    )
    wave_rows = wave_rows.reshape(level_dev, 2, lat_rows, waves, 2)
    fourier = to_slots(wave_rows, wave_of_slot, in_use)
    owned_fourier = lax.all_to_all(
        fourier.astype(jnp.bfloat16), "lat", split_axis=3, concat_axis=2, tiled=True
    )
    blocks = owned_fourier.reshape(level_dev, 2, latitudes, capacity, 2)
    halves = jnp.stack([blocks[:, :, :half_lat], jnp.flip(blocks[:, :, half_lat:], axis=2)], axis=0)
    degree_ids = jnp.arange(degrees, dtype=jnp.int32)
    parity = jnp.where(degree_ids % 2 == 0, 1.0, -1.0).astype(jnp.float32)
    both_sums = jnp.einsum("plfasr,sja->pslfrj", halves, basis, preferred_element_type=jnp.float32)
    raw_coeffs = (both_sums[0] + parity * both_sums[1]) * (1.0 / math.sqrt(latitudes))
    wave_here = lax.dynamic_slice_in_dim(wave_of_slot, owner_index * capacity, capacity)
    count_here = lax.dynamic_slice_in_dim(count_of_slot, owner_index * capacity, capacity)
    level_rates = lax.dynamic_slice_in_dim(viscosity, sector_index * level_dev, level_dev)
    total_degree = wave_here[:, None] + degree_ids[None, :]
    scaled = (total_degree * (total_degree + 1)).astype(jnp.float32) / float(
        degrees * (degrees + 1)
    )
    damping = 1.0 / (
        1.0 + level_rates[None, :, None, None, None] * (scaled * scaled)[:, None, None, None, :]
    )
    kept_mask = degree_ids[None, :] < count_here[:, None]
    spectral = jnp.where(kept_mask[:, None, None, None, :], raw_coeffs * damping, jnp.float32(0.0))
    rounded = spectral.astype(jnp.bfloat16)
    signed = rounded * parity.astype(jnp.bfloat16)
    both_back = jnp.einsum(
        "pslfrj,sja->plfasr",
        jnp.stack([rounded, signed], axis=0),
        basis,
        preferred_element_type=jnp.float32,
    )
    returned = jnp.concatenate([both_back[0], jnp.flip(both_back[1], axis=2)], axis=2) * (
        1.0 / math.sqrt(degrees)
    )
    returned = returned.astype(jnp.bfloat16).reshape(level_dev, 2, latitudes, 2 * capacity)
    regrouped = lax.all_to_all(returned, "lat", split_axis=2, concat_axis=3, tiled=True)
    grid_lines = from_slots(regrouped, wave_slots, table)
    tendency = lax.all_to_all(grid_lines, "lon", split_axis=3, concat_axis=0, tiled=True)
    return (spectral, tendency)


def solution(mesh):
    return jax.shard_map(
        body,
        mesh=mesh,
        in_specs=(
            P(None, "lat", "lon"),
            P(None, "lat", "lon"),
            P("lat", None, None),
            P(),
            P(),
            P(),
        ),
        out_specs=(P("lat", "lon", None, None, None), P(None, None, "lat", "lon")),
        check_vma=False,
    )
```

profile of v0, /device:TPU:2, one launch (start us, length us, event | category | flops | bytes accessed | tf_op | source)
XLA Modules:
  0.0 278.3 jit_solution(4374377458167274083)
XLA Ops:
  0.6 1.1 multiply_bitcast_fusion.1
  2.5 7.1 %all-to-all-start = ((f32[8,2,16,320]{3,2,1,0:T(8,128)}), f32[8,2,16,320]{3,2,1,0:T(8,128)S(1)}, u32[]{:S(2)}, u32[]{:S(2)}) async-start(f32[8,2,16,320]{3,2,1,0:T(8,128)} %pad_maximum_fusion.1), calls=%async_computation | async-start | bytes 786432 | tf_op jit(solution)/shard_map/all_to_all | solution.py:61
  9.6 28.1 %negate_multiply_fusion = (f32[2560,640,1]{1,0,2:T(8,128)}, f32[2560,640,1]{1,0,2:T(8,128)}) fusion(), kind=kLoop, calls=%fused_computation.15 | loop fusion | flops 19660800 | bytes 13107200 | tf_op jit(solution)/shard_map/mul | solution.py:15
  38.8 10.3 %pad_maximum_fusion = f32[2560,640,2]{1,0,2:T(8,128)} fusion(f32[2560,640,1]{1,0,2:T(8,128)} %get-tuple-element.26, f32[2560,640,1]{1,0,2:T(8,128)} %get-tuple-element.27), kind=kLoop, calls=%fused_computation.2 | loop fusion | flops 3276800 | bytes 26214400 | tf_op jit(solution)/shard_map/stack | solution.py:15
  49.2 20.2 %copy.105 = f32[2560,640,2]{0,2,1:T(2,128)} copy(f32[2560,640,2]{1,0,2:T(8,128)} %pad_maximum_fusion) | data formatting | bytes 26214400 | tf_op jit(solution)/shard_map/stack | solution.py:15
  69.4 16.2 %reshape.343 = f32[2560,1280]{0,1:T(8,128)} reshape(f32[2560,640,2]{0,2,1:T(2,128)} %copy.105) | data formatting | bytes 26214400 | tf_op jit(solution)/shard_map/reshape | solution.py:16
  85.6 15.7 %dot_general.29 = f32[640,2,2560]{2,1,0:T(2,128)} reshape(f32[1280,2560]{1,0:T(8,128)} %bitcast.106) | data formatting | bytes 26214400 | tf_op jit(solution)/shard_map/dot_general | solution.py:63
  103.5 15.8 %fusion.2 = bf16[2,16,640,2]{2,1,3,0:T(8,128)(2,1)S(1)} fusion(f32[640,2,2560]{2,1,0:T(2,128)} %dot_general.29, f32[2,16,2560,1]{2,1,0,3:T(8,128)S(1)} %reshape.373), kind=kOutput, calls=%fused_computation.5 | convolution fusion | flops 1258291200 | bytes 13516800 | tf_op jit(solution)/shard_map/dot_general | solution.py:63
  119.7 4.4 %gather_fusion = bf16[864,2,16,2]{2,3,1,0:T(2,128)(2,1)S(1)} fusion(bf16[2,16,640,2]{1,3,2,0:T(2,128)(2,1)S(1)} %copy.107, s32[1024]{0:T(1024)S(1)} %pad_clamp_fusion.1), kind=kCustom, calls=%fused_computation | custom fusion | bytes 224640 | tf_op jit(solution)/shard_map/jit(_take)/gather | solution.py:20
  125.1 1.4 copy.110
  126.4 1.5 reshape.380
  127.9 19.1 %all-to-all-start.1 = ((bf16[96,2,288]{2,1,0:T(2,128)(2,1)}), bf16[96,2,288]{2,1,0:T(2,128)(2,1)S(1)}, u32[]{:S(2)}, u32[]{:S(2)}) async-start(bf16[96,2,288]{2,1,0:T(2,128)(2,1)} %reshape.380), calls=%async_computation.1 | async-start | bytes 294912 | tf_op jit(solution)/shard_map/all_to_all | solution.py:71
  147.8 14.1 %all-to-all-done.1 = bf16[96,2,288]{2,1,0:T(2,128)(2,1)S(1)} async-done(((bf16[96,2,288]{2,1,0:T(2,128)(2,1)}), bf16[96,2,288]{2,1,0:T(2,128)(2,1)S(1)}, u32[]{:S(2)}, u32[]{:S(2)}) %all-to-all-start.1) | async-done | bytes 110624 | tf_op jit(solution)/shard_map/all_to_all | solution.py:71
  161.8 0.9 reshape.381
  162.9 0.9 reshape.344
  164.8 6.0 %fusion.22 = f32[2,9,1,2,2,640]{5,4,3,0,1,2:T(2,128)S(1)} fusion(bf16[9,640,768]{2,1,0:T(8,128)(2,1)} %param.8, bf16[1,1,2,768,9,2]{3,5,2,0,4,1:T(2,128)(2,1)S(1)} %bitcast.121, bf16[1,1,2,768,9,2]{3,5,2,0,4,1:T(2,128)(2,1)S(1)} %bitcast.122), kind=kOutput, calls=%fused_computation.30 | convolution fusion | flops 71000064 | bytes 9142272 | tf_op jit(solution)/shard_map/plfasr,sja->pslfrj/dot_general | solution.py:78
  170.9 4.9 %fusion.19 = f32[2,1,2,768,9,2]{3,5,2,0,4,1:T(2,128)S(1)} fusion(bf16[9,640,768]{2,1,0:T(8,128)(2,1)} %param.8, bf16[1,9,1,2,2,640]{5,4,3,0,1,2:T(2,128)(2,1)S(1)} %get-tuple-element.18, bf16[1,9,1,2,2,640]{5,4,3,0,1,2:T(2,128)(2,1)S(1)} %get-tuple-element.19), kind=kOutput, calls=%fused_computation.29 | convolution fusion | flops 70963200 | bytes 9160704 | tf_op jit(solution)/shard_map/pslfrj,sja->plfasr/dot_general | solution.py:94
  177.6 1.7 reshape.382
  179.3 16.7 %all-to-all-start.2 = ((bf16[96,2,288]{2,1,0:T(2,128)(2,1)}), bf16[96,2,288]{2,1,0:T(2,128)(2,1)S(1)}, u32[]{:S(2)}, u32[]{:S(2)}) async-start(bf16[96,2,288]{2,1,0:T(2,128)(2,1)} %reshape.382), calls=%async_computation.2 | async-start | bytes 294912 | tf_op jit(solution)/shard_map/all_to_all | solution.py:104
  196.0 14.8 %all-to-all-done.2 = bf16[96,2,288]{2,1,0:T(2,128)(2,1)S(1)} async-done(((bf16[96,2,288]{2,1,0:T(2,128)(2,1)}), bf16[96,2,288]{2,1,0:T(2,128)(2,1)S(1)}, u32[]{:S(2)}, u32[]{:S(2)}) %all-to-all-start.2) | async-done | bytes 110624 | tf_op jit(solution)/shard_map/all_to_all | solution.py:104
  210.8 1.1 reshape.383
  211.9 2.2 copy.130
  215.2 3.3 %gather_fusion.1 = bf16[640,2,16,2]{2,3,1,0:T(2,128)(2,1)S(1)} fusion(bf16[2,16,864,2]{1,3,2,0:T(2,128)(2,1)S(1)} %copy.120, s32[1024]{0:T(1024)S(1)} %pad_clamp_fusion), kind=kCustom, calls=%fused_computation.1 | custom fusion | bytes 166400 | tf_op jit(solution)/shard_map/jit(_take)/gather | solution.py:30
  218.5 3.3 %multiply_bitcast_fusion = f32[2,16,640,2]{1,3,0,2:T(2,128)S(1)} fusion(f32[640]{0:T(1024)S(1)} %fusion.47, bf16[640,2,16,2]{2,3,1,0:T(2,128)(2,1)S(1)} %gather_fusion.1, pred[640]{0:T(1024)(128)(4,1)S(1)} %compare_and_fusion), kind=kLoop, calls=%fused_computation.27 | loop fusion | flops 122880 | bytes 248960 | tf_op jit(solution)/shard_map/mul | solution.py:32
  221.8 23.5 %fusion.14 = f32[1,2,16,2560]{3,2,1,0:T(8,128)S(1)} fusion(f32[2,16,640,2]{1,3,0,2:T(2,128)S(1)} %multiply_bitcast_fusion, f32[2560,640,1]{1,0,2:T(8,128)} %get-tuple-element.26, f32[2560,640,1]{1,0,2:T(8,128)} %get-tuple-element.27), kind=kOutput, calls=%fused_computation.21 | convolution fusion | flops 1261568000 | bytes 13598720 | tf_op jit(solution)/shard_map/dot_general | solution.py:33
  245.2 1.4 copy.122
  246.7 4.2 %reshape.384 = f32[8,1,10240]{2,1,0:T(1,128)} reshape(f32[2560,1,2,16]{3,2,1,0:T(2,128)S(1)} %bitcast.107) | data formatting | bytes 655360
  250.9 7.2 %all-to-all-start.3 = ((f32[8,1,10240]{2,1,0:T(1,128)}), f32[8,1,10240]{2,1,0:T(1,128)S(1)}, u32[]{:S(2)}, u32[]{:S(2)}) async-start(f32[8,1,10240]{2,1,0:T(1,128)} %reshape.384), calls=%async_computation.3 | async-start | bytes 655360 | tf_op jit(solution)/shard_map/all_to_all | solution.py:106
  258.8 11.7 %all-to-all-done.3 = f32[8,1,10240]{2,1,0:T(1,128)S(1)} async-done(((f32[8,1,10240]{2,1,0:T(1,128)}), f32[8,1,10240]{2,1,0:T(1,128)S(1)}, u32[]{:S(2)}, u32[]{:S(2)}) %all-to-all-start.3) | async-done | bytes 327712 | tf_op jit(solution)/shard_map/all_to_all | solution.py:106
  271.0 1.4 reduce.2
  272.4 3.5 %reshape.385 = f32[2560,1,2,16]{3,2,1,0:T(2,128)S(1)} reshape(f32[8,10240]{1,0:T(8,128)S(1)} %reduce.2) | data formatting | bytes 655360
  275.9 2.2 copy.123
  (49 shorter events, 11.5 us)
Async XLA Ops:
  2.5 100.7 %all-to-all-start = ((f32[8,2,16,320]{3,2,1,0:T(8,128)}), f32[8,2,16,320]{3,2,1,0:T(8,128)S(1)}, u32[]{:S(2)}, u32[]{:S(2)}) async-start(f32[8,2,16,320]{3,2,1,0:T(8,128)} %pad_maximum_fusion.1), calls=%async_computation | async-start | bytes 786432 | tf_op jit(solution)/shard_map/all_to_all | solution.py:61
  9.6 28.1 %copy-start = (s32[640]{0:T(1024)S(1)}, s32[640]{0:T(1024)}, u32[]{:S(2)}) copy-start(s32[640]{0:T(1024)} %param.9) | copy-start | bytes 7684
  9.6 28.1 %copy-start.1 = (s32[640]{0:T(1024)S(1)}, s32[640]{0:T(1024)}, u32[]{:S(2)}) copy-start(s32[640]{0:T(1024)} %param.10) | copy-start | bytes 7684
  85.6 16.8 %copy-start.2 = (f32[8]{0:T(128)S(1)}, f32[8]{0:T(128)}, u32[]{:S(2)}) copy-start(f32[8]{0:T(128)} %param.11) | copy-start | bytes 100
  127.9 33.9 %all-to-all-start.1 = ((bf16[96,2,288]{2,1,0:T(2,128)(2,1)}), bf16[96,2,288]{2,1,0:T(2,128)(2,1)S(1)}, u32[]{:S(2)}, u32[]{:S(2)}) async-start(bf16[96,2,288]{2,1,0:T(2,128)(2,1)} %reshape.380), calls=%async_computation.1 | async-start | bytes 294912 | tf_op jit(solution)/shard_map/all_to_all | solution.py:71
  179.3 31.5 %all-to-all-start.2 = ((bf16[96,2,288]{2,1,0:T(2,128)(2,1)}), bf16[96,2,288]{2,1,0:T(2,128)(2,1)S(1)}, u32[]{:S(2)}, u32[]{:S(2)}) async-start(bf16[96,2,288]{2,1,0:T(2,128)(2,1)} %reshape.382), calls=%async_computation.2 | async-start | bytes 294912 | tf_op jit(solution)/shard_map/all_to_all | solution.py:104
  250.9 19.6 %all-to-all-start.3 = ((f32[8,1,10240]{2,1,0:T(1,128)}), f32[8,1,10240]{2,1,0:T(1,128)S(1)}, u32[]{:S(2)}, u32[]{:S(2)}) async-start(f32[8,1,10240]{2,1,0:T(1,128)} %reshape.384), calls=%async_computation.3 | async-start | bytes 655360 | tf_op jit(solution)/shard_map/all_to_all | solution.py:106
where the time goes:
time: 284 us; the launch traced here: 278 us
  local copies, waits for them, and re-layouts  88.5 us (31%)
  matrix products  50.1 us (18%)
  starting transfers between devices  50 us (18%)
  other arithmetic  47.9 us (17%)
  waiting for transfers between devices  40.5 us (14%)
    mul x1, other arithmetic, wave_table(): -jnp.sin(angles) * scaling  28.1 us
    dot_general x1, matrix products, from_slots(): lax.dot_general(weighted, table, (((1,), (1,)), ((), ())), precision=lax....  23.5 us
    another operation x1, local copies, waits for them, and re-layouts, wave_table(): jnp.stack([jnp.cos(angles) * scaling, -jnp.sin(angles) * scaling], axis=2)  20.2 us
    all_to_all x1, starting transfers between devices, body(): lax.all_to_all(fourier.astype(jnp.bfloat16), 'lat', split_axis=3, concat_...  19.1 us
    all_to_all x1, starting transfers between devices, body(): lax.all_to_all(returned, 'lat', split_axis=2, concat_axis=3, tiled=True)  16.7 us
    reshape x1, local copies, waits for them, and re-layouts, wave_table(): return stacked.reshape(col_count, 2 * waves)  16.2 us
    dot_general x2, local copies, waits for them, and re-layouts, body(): jnp.dot(lon_lines.reshape(-1, full_length), table, precision=lax.Precisio...  16.2 us
    dot_general x1, matrix products, body(): jnp.dot(lon_lines.reshape(-1, full_length), table, precision=lax.Precisio...  15.8 us
  transfers between devices with their start and end apart: 4, of which 3 were waited for; matrix products, arithmetic and copies ran while one was open for 34% of the time, Pallas kernels for 0%

commit v1 on v0

v1 whole, which is shorter than its diff:
```python
import functools
import math

import jax
import jax.numpy as jnp
import ml_dtypes
import numpy as np
from jax import lax
from jax.experimental import pallas as pl
from jax.experimental.pallas import tpu as pltpu
from jax.sharding import PartitionSpec as P

MESH = pl.DeviceIdType.MESH
F32 = jnp.float32
BF16 = jnp.bfloat16

NX, NZ, NC = 4, 12, 2
GROUPS = NX * NC
SECTORS = 8
ROWS = 48
HALF = math.sqrt(0.5)


def nt(a, b):
    return lax.dot_general(a, b, (((1,), (1,)), ((), ())), preferred_element_type=F32)


def nn(a, b):
    return lax.dot_general(a, b, (((1,), (0,)), ((), ())), preferred_element_type=F32)


def tn(a, b):
    return lax.dot_general(a, b, (((0,), (0,)), ((), ())), preferred_element_type=F32)


@functools.cache
def wave_lanes(waves):
    per = waves // SECTORS
    out = np.full((4, 256), -1, np.int64)
    for j in range(4):
        other = 4 if j == 0 else SECTORS - j
        out[j, :per] = SECTORS * np.arange(per) + j
        out[j, per : 2 * per] = SECTORS * np.arange(per) + other
    return out


@functools.cache
def dft_table(length, waves):
    sector = length // SECTORS
    per = waves // SECTORS
    lanes = wave_lanes(waves)
    t = np.arange(sector)
    table = np.zeros((4, 2, sector, 2, 256), np.float64)
    for j in range(4):
        m = lanes[j, : 2 * per]
        angle = 2.0 * math.pi * ((t[:, None] * m[None, :]) % length) / length
        c, s = np.cos(angle), np.sin(angle)
        if j == 0:
            table[j, 0, :, 0, :per] = c[:, :per]
            table[j, 0, :, 1, :per] = -s[:, :per]
            table[j, 1, :, 0, per : 2 * per] = c[:, per:]
            table[j, 1, :, 1, per : 2 * per] = -s[:, per:]
        else:
            sign = np.where(np.arange(2 * per) < per, 1.0, -1.0)
            table[j, 0, :, 0, : 2 * per] = c
            table[j, 0, :, 1, : 2 * per] = -s
            table[j, 1, :, 0, : 2 * per] = s * sign
            table[j, 1, :, 1, : 2 * per] = c * sign
    table = table.reshape(4, 2 * sector, 512) / math.sqrt(length)
    high = table.astype(ml_dtypes.bfloat16)
    low = (table - high.astype(np.float64)).astype(ml_dtypes.bfloat16)
    return high, low


@functools.cache
def spread_table(cap):
    e = np.zeros((NZ, ROWS, 4, 128), np.float32)
    for z in range(NZ):
        for k in range(cap):
            for f in range(2):
                for r in range(2):
                    e[z, k * 4 + f * 2 + r, r * 2 + f, z * cap + k] = 1.0
    return e.reshape(NZ * ROWS, 512).astype(ml_dtypes.bfloat16)


@functools.cache
def lane_table():
    p = np.zeros((512, 512), np.float32)
    for z in range(4):
        for x in range(NX):
            for c in range(NC):
                for i in range(16):
                    lane = z * 32 + c * 16 + i
                    if x >= NX // 2:
                        lane = 127 - lane
                    p[z * 128 + (x * NC + c) * 16 + i, x * 128 + lane] = 1.0
    return p.astype(ml_dtypes.bfloat16)


def kernel(
    u_ref, v_ref, tgt_ref, ws_ref, cnt_ref, visc_ref, basis_hbm, hi_hbm, lo_hbm, e_hbm, pi_hbm,
    spec_ref, tend_ref,
    basis, hi, lo, e_tab, pi_tab, onehot, damp,
    send_l, recv_l, send_a, recv_a, send_b, recv_b, turned,
    back_t, send_b2, recv_b2, send_a2, recv_a2, send_l2, recv_l2,
    load_sem, sl, rl, sa, ra, sb, rb, sb2, rb2, sa2, ra2, sl2, rl2,
):
    lat = lax.axis_index("lat")
    lon = lax.axis_index("lon")
    x = lat // (NZ * NC)
    z = lat // NC % NZ
    core = lat % NC
    group = x * NC + core
    cap, degrees, half_lat = basis.shape
    waves = ws_ref.shape[1]
    sector = u_ref.shape[2]

    def in_group(g):
        return ((g // NC) * (NZ * NC) + z * NC + g % NC, lon)

    def in_column(zz):
        return (x * (NZ * NC) + zz * NC + core, lon)

    def in_sector(s):
        return (lat, s)

    barrier = pltpu.get_barrier_semaphore()

    def greet(device_of, me, n):
        def one(d, carry):
            pl.semaphore_signal(barrier, inc=1, device_id=device_of((me + d) % n), device_id_type=MESH)
            return carry

        lax.fori_loop(1, n, one, 0)

    greet(in_sector, lon, SECTORS)
    greet(in_group, group, GROUPS)
    greet(in_column, z, NZ)

    loads = [
        pltpu.make_async_copy(src, dst, load_sem.at[i])
        for i, (src, dst) in enumerate(
            ((hi_hbm, hi), (lo_hbm, lo), (e_hbm, e_tab), (pi_hbm, pi_tab), (basis_hbm, basis))
        )
    ]
    for load in loads:
        load.start()

    def products(level, carry):
        u = u_ref[level]
        v = v_ref[level]
        send_l[level, 0] = u * v
        send_l[level, 1] = u * u - v * v
        return carry

    lax.fori_loop(0, SECTORS, products, 0)
    recv_l[lon] = send_l[lon]
    pl.semaphore_wait(barrier, SECTORS + GROUPS + NZ - 3)

    def exchange(src, dst, send_sem, recv_sem, device_of, me, n):
        def copy(d):
            to = (me + d) % n
            return pltpu.make_async_remote_copy(
                src_ref=src.at[to],
                dst_ref=dst.at[me],
                send_sem=send_sem.at[d],
                recv_sem=recv_sem.at[d],
                device_id=device_of(to),
                device_id_type=MESH,
            )

        def start():
            def one(d, carry):
                copy(d).start()
                return carry

            lax.fori_loop(1, n, one, 0)

        def wait():
            def one(d, carry):
                copy(d).wait()
                return carry

            lax.fori_loop(1, n, one, 0)

        return start, wait

    start, wait = exchange(send_l, recv_l, sl, rl, in_sector, lon, SECTORS)
    start()

    target = tgt_ref[...]
    for b in range(GROUPS):
        ids = lax.broadcasted_iota(jnp.int32, (128, 1024), 0) + b * 128
        onehot[pl.ds(b * 128, 128), :] = jnp.where(ids == target, 1.0, 0.0).astype(BF16)

    rows40 = damp.shape[0]
    slot = lax.broadcasted_iota(jnp.int32, (rows40, waves), 0) // 4
    here = (ws_ref[...] == lat * cap + slot) & (slot < cap)
    wave_ids = lax.broadcasted_iota(jnp.int32, (rows40, waves), 1)
    wave_here = jnp.sum(jnp.where(here, wave_ids, 0).astype(F32), axis=1, keepdims=True)
    kept_here = jnp.sum(jnp.where(here, cnt_ref[...], 0).astype(F32), axis=1, keepdims=True)
    levels = lax.broadcasted_iota(jnp.int32, (1, SECTORS), 1)
    rate = jnp.sum(jnp.where(levels == lon, visc_ref[...], 0.0), axis=1, keepdims=True)
    degree = lax.broadcasted_iota(jnp.int32, (rows40, degrees), 1).astype(F32)
    total = wave_here + degree
    q = total * (total + 1.0) / float(degrees * (degrees + 1))
    damping = (1.0 / math.sqrt(2 * half_lat)) / (1.0 + rate * (q * q))
    damp[...] = jnp.where(degree < kept_here, damping, 0.0)

    wait()
    loads[0].wait()
    loads[1].wait()

    sums = []
    for f in range(2):
        a = [recv_l[s, f] for s in range(SECTORS)]
        e0, e1, e2, e3 = (a[i] + a[i + 4] for i in range(4))
        o0, o1, o2, o3 = (a[i] - a[i + 4] for i in range(4))
        od = HALF * (o1 - o3)
        os = HALF * (o1 + o3)
        sums.append(
            (
                (e0 + e1 + e2 + e3, e0 - e1 + e2 - e3),
                (o0 + od, -(os + o2)),
                (e0 - e2, e3 - e1),
                (o0 - od, o2 - os),
            )
        )
    for j in range(4):
        both = jnp.concatenate(
            [jnp.concatenate([sums[f][j][0], sums[f][j][1]], axis=1) for f in range(2)], axis=0
        )
        high = both.astype(BF16)
        low = (both - high.astype(F32)).astype(BF16)
        two = nn(jnp.concatenate([high, low], axis=0), hi[j])
        four = two[:32] + two[32:] + nn(high, lo[j])
        turned[0:32, pl.ds(j * 256, 256)] = four[:, :256].astype(BF16)
        turned[32:64, pl.ds(j * 256, 256)] = four[:, 256:].astype(BF16)

    placed = nt(turned[...], onehot[...]).astype(BF16)
    for g in range(GROUPS):
        for b in range(4):
            send_a[g, :, pl.ds(b * 128, 128)] = placed[b * 16 : b * 16 + 16, g * 128 : g * 128 + 128]
    start, wait = exchange(send_a, recv_a, sa, ra, in_group, group, GROUPS)
    start()
    recv_a[group] = send_a[group]
    loads[2].wait()
    wait()
    spread = nt(e_tab[...], recv_a[...].reshape(GROUPS * 16, 512)).astype(BF16)
    send_b[...] = spread.reshape(NZ, ROWS, 128)
    start, wait = exchange(send_b, recv_b, sb, rb, in_column, z, NZ)
    start()
    recv_b[z] = send_b[z]
    loads[3].wait()
    loads[4].wait()
    wait()

    quarters = NZ // 4
    gathered = jnp.concatenate(
        [
            jnp.concatenate([recv_b[4 * i + k] for k in range(4)], axis=1)
            for i in range(quarters)
        ],
        axis=0,
    )
    natural = nn(gathered, pi_tab[...])
    parity = jnp.where(lax.broadcasted_iota(jnp.int32, (8, degrees), 1) % 2 == 0, 1.0, -1.0)
    first = lax.broadcasted_iota(jnp.int32, (8, 1), 0) < 4
    blocks = half_lat // 128
    for i in range((cap + 1) // 2):
        r0 = 8 * i
        north, south = [], []
        for b in range(blocks):
            xx, gg = b // quarters, b % quarters
            north.append(natural[gg * ROWS + r0 : gg * ROWS + r0 + 8, xx * 128 : xx * 128 + 128])
            xx, gg = NX - 1 - xx, quarters - 1 - gg
            south.append(natural[gg * ROWS + r0 : gg * ROWS + r0 + 8, xx * 128 : xx * 128 + 128])
        both = jnp.concatenate(
            [jnp.concatenate(north, axis=1), jnp.concatenate(south, axis=1)], axis=0
        ).astype(BF16)
        raws = []
        for k in (2 * i, 2 * i + 1):
            if k < cap:
                out = nt(both, basis[k])
                raws.append(out[:8] + parity * out[8:])
        raw = jnp.where(first, raws[0], raws[1] if len(raws) > 1 else 0.0)
        spectral = raw * damp[pl.ds(r0, 8), :]
        for k in (2 * i, 2 * i + 1):
            if k < cap:
                at = 4 * (k - 2 * i)
                for f in range(2):
                    spec_ref[k, 0, f] = spectral[at + 2 * f : at + 2 * f + 2]
        rounded = spectral.astype(BF16).astype(F32)
        pair = jnp.concatenate([rounded, rounded * parity], axis=0).astype(BF16)
        outs = [nn(pair, basis[k]) for k in (2 * i, 2 * i + 1) if k < cap]
        keep = jnp.concatenate([first, first], axis=0)
        back = jnp.where(keep, outs[0], outs[1] if len(outs) > 1 else 0.0)
        back = back * (1.0 / math.sqrt(degrees))
        for b in range(blocks):
            xx, gg = b // quarters, b % quarters
            back_t[pl.ds(gg * ROWS + r0, 8), pl.ds(xx * 128, 128)] = back[:8, b * 128 : b * 128 + 128]
            xx, gg = NX - 1 - xx, quarters - 1 - gg
            back_t[pl.ds(gg * ROWS + r0, 8), pl.ds(xx * 128, 128)] = back[8:, b * 128 : b * 128 + 128]
    for gg in range(quarters):
        back_t[pl.ds(gg * ROWS + 40, 8), :] = jnp.zeros((8, 512), F32)

    mixed = nt(back_t[...].astype(BF16), pi_tab[...]).astype(BF16)
    for zz in range(NZ):
        send_b2[zz] = mixed[zz // 4 * ROWS : zz // 4 * ROWS + ROWS, zz % 4 * 128 : zz % 4 * 128 + 128]
    start, wait = exchange(send_b2, recv_b2, sb2, rb2, in_column, z, NZ)
    start()
    recv_b2[z] = send_b2[z]
    wait()
    joined = tn(recv_b2[...].reshape(NZ * ROWS, 128), e_tab[...]).astype(BF16)
    send_a2[...] = joined.reshape(GROUPS, 16, 512)
    start, wait = exchange(send_a2, recv_a2, sa2, ra2, in_group, group, GROUPS)
    start()
    recv_a2[group] = send_a2[group]
    wait()

    by_part = jnp.concatenate(
        [
            jnp.concatenate([recv_a2[g, :, pl.ds(b * 128, 128)] for g in range(GROUPS)], axis=1)
            for b in range(4)
        ],
        axis=0,
    )
    waved = nn(by_part, onehot[...])
    weight = jnp.where(lax.broadcasted_iota(jnp.int32, (1, 1024), 1) == 0, 1.0, 2.0)
    waved = (waved * weight).astype(BF16)
    parts = []
    for j in range(4):
        lhs = jnp.concatenate(
            [waved[:32, j * 256 : j * 256 + 256], waved[32:, j * 256 : j * 256 + 256]], axis=1
        )
        out = nt(lhs, hi[j]) + nt(lhs, lo[j])
        parts.append((out[:, :sector], out[:, sector:]))
    (u0, u4), (u1, v1), (u2, v2), (u3, v3) = parts
    even, odd = u0 + u4, u0 - u4
    ud, us = HALF * (u1 - u3), u1 + u3
    vd, vs = v1 - v3, HALF * (v1 + v3)
    grid = (
        even + us + u2,
        odd + ud - vs - v2,
        even - u2 - vd,
        odd - ud - vs + v2,
        even - us + u2,
        odd - ud + vs - v2,
        even - u2 + vd,
        odd + ud + vs + v2,
    )
    for s in range(SECTORS):
        send_l2[s] = grid[s].astype(BF16)
    start, wait = exchange(send_l2, recv_l2, sl2, rl2, in_sector, lon, SECTORS)
    start()
    recv_l2[lon] = send_l2[lon]
    wait()
    for s in range(SECTORS):
        tend_ref[s] = recv_l2[s].astype(F32).reshape(2, 16, sector)


def body(wind_u, wind_v, basis, wave_slots, degree_count, viscosity):
    levels, lat_rows, sector = wind_u.shape
    cap, degrees, half_lat = basis.shape
    waves = wave_slots.shape[0]
    per = waves // SECTORS
    high, low = dft_table(sector * SECTORS, waves)
    owner = wave_slots // cap
    lane = (owner // (NZ * NC) * NC + owner % NC) * 128 + owner // NC % NZ * cap + wave_slots % cap
    by_residue = lane.reshape(per, SECTORS).T
    fill = jnp.full((256 - 2 * per,), -1, jnp.int32)
    target = jnp.concatenate(
        [
            part
            for j in range(4)
            for part in (by_residue[j], by_residue[4 if j == 0 else SECTORS - j], fill)
        ]
    ).reshape(1, 1024)
    vmem = pl.BlockSpec(memory_space=pltpu.VMEM)
    hbm = pl.BlockSpec(memory_space=pl.ANY)
    dma = pltpu.SemaphoreType.DMA
    return pl.pallas_call(
        kernel,
        out_shape=(
            jax.ShapeDtypeStruct((cap, 1, 2, 2, degrees), F32),
            jax.ShapeDtypeStruct((levels, 2, lat_rows, sector), F32),
        ),
        in_specs=[vmem] * 6 + [hbm] * 5,
        out_specs=(vmem, vmem),
        scratch_shapes=[
            pltpu.VMEM(basis.shape, BF16),
            pltpu.VMEM(high.shape, BF16),
            pltpu.VMEM(low.shape, BF16),
            pltpu.VMEM((NZ * ROWS, 512), BF16),
            pltpu.VMEM((512, 512), BF16),
            pltpu.VMEM((1024, 1024), BF16),
            pltpu.VMEM((40, degrees), F32),
            pltpu.VMEM((SECTORS, 2, lat_rows, sector), F32),
            pltpu.VMEM((SECTORS, 2, lat_rows, sector), F32),
            pltpu.VMEM((GROUPS, 16, 512), BF16),
            pltpu.VMEM((GROUPS, 16, 512), BF16),
            pltpu.VMEM((NZ, ROWS, 128), BF16),
            pltpu.VMEM((NZ, ROWS, 128), BF16),
            pltpu.VMEM((64, 1024), BF16),
            pltpu.VMEM((NZ // 4 * ROWS, 512), F32),
            pltpu.VMEM((NZ, ROWS, 128), BF16),
            pltpu.VMEM((NZ, ROWS, 128), BF16),
            pltpu.VMEM((GROUPS, 16, 512), BF16),
            pltpu.VMEM((GROUPS, 16, 512), BF16),
            pltpu.VMEM((SECTORS, 2 * lat_rows, sector), BF16),
            pltpu.VMEM((SECTORS, 2 * lat_rows, sector), BF16),
            dma((5,)),
        ]
        + [dma((n,)) for n in (8, 8, 8, 8, 12, 12, 12, 12, 8, 8, 8, 8)],
        compiler_params=pltpu.CompilerParams(
            collective_id=0, has_side_effects=True, vmem_limit_bytes=48 * 2**20
        ),
    )(
        wind_u,
        wind_v,
        target,
        wave_slots.reshape(1, waves),
        degree_count.reshape(1, waves),
        viscosity.reshape(1, levels),
        basis,
        jnp.asarray(high),
        jnp.asarray(low),
        jnp.asarray(spread_table(cap)),
        jnp.asarray(lane_table()),
    )


def solution(mesh):
    return jax.shard_map(
        body,
        mesh=mesh,
        in_specs=(
            P(None, "lat", "lon"),
            P(None, "lat", "lon"),
            P("lat", None, None),
            P(),
            P(),
            P(),
        ),
        out_specs=(P("lat", "lon", None, None, None), P(None, None, "lat", "lon")),
        check_vma=False,
    )
```

time: 284 us -> 81.1 us (0.29)
  the two profiles are of different devices: /device:TPU:2 before, /device:TPU:1 now
where the time goes in v1:
time: 81.1 us; the launch traced here: 80.2 us
  Pallas kernels  69.2 us (85%)
  local copies, waits for them, and re-layouts  9.63 us (12%)
    pallas_call x1, Pallas kernels, body(): pl.pallas_call(kernel, out_shape=(jax.ShapeDtypeStruct((cap, 1, 2, 2, deg...  69.2 us
    unnamed x14, local copies, waits for them, and re-layouts  7.74 us

profile of v1, /device:TPU:1, one launch (start us, length us, event | category | flops | bytes accessed | tf_op | source)
XLA Modules:
  0.0 80.2 jit_solution(14763349320591609822)
XLA Ops:
  0.6 0.7 reshape.22.cnt_ref
  1.3 0.7 reshape.21.ws_ref
  2.0 0.7 fusion.4
  2.7 0.1 reshape.19
  2.8 0.3 slice_reduce_fusion
  3.2 0.1 concatenate.3
  3.3 0.0 copy-start
  3.3 1.7 %copy-done = bf16[4,640,512]{2,1,0:T(8,128)(2,1)S(1)} copy-done((bf16[4,640,512]{2,1,0:T(8,128)(2,1)S(1)}, bf16[4,640,512]{2,1,0:T(8,128)(2,1)}, u32[]{:S(2)}) %copy-start) | copy-done | bytes 2621464
  5.0 0.0 copy-start.1
  5.0 1.1 %copy-done.1 = bf16[576,512]{1,0:T(8,128)(2,1)S(1)} copy-done((bf16[576,512]{1,0:T(8,128)(2,1)S(1)}, bf16[576,512]{1,0:T(8,128)(2,1)}, u32[]{:S(2)}) %copy-start.1) | copy-done | bytes 589848
  6.1 0.0 copy-start.2
  6.1 1.0 %copy-done.2 = bf16[512,512]{1,0:T(8,128)(2,1)S(1)} copy-done((bf16[512,512]{1,0:T(8,128)(2,1)S(1)}, bf16[512,512]{1,0:T(8,128)(2,1)}, u32[]{:S(2)}) %copy-start.2) | copy-done | bytes 524312
  7.1 0.0 copy-start.3
  7.1 0.9 %copy-done.3 = f32[8,16,320]{2,1,0:T(8,128)S(1)} copy-done((f32[8,16,320]{2,1,0:T(8,128)S(1)}, f32[8,16,320]{2,1,0:T(8,128)}, u32[]{:S(2)}) %copy-start.3) | copy-done | bytes 163864
  8.0 0.0 copy-start.4
  8.0 0.9 %copy-done.4 = f32[8,16,320]{2,1,0:T(8,128)S(1)} copy-done((f32[8,16,320]{2,1,0:T(8,128)S(1)}, f32[8,16,320]{2,1,0:T(8,128)}, u32[]{:S(2)}) %copy-start.4) | copy-done | bytes 163864
  9.0 0.0 copy-start.5
  9.0 0.7 copy-done.5
  9.6 69.2 %shard_map.113 = (f32[9,1,2,2,640]{4,3,2,1,0:T(2,128)S(1)}, f32[8,2,16,320]{3,2,1,0:T(8,128)S(1)}) custom-call(f32[8,16,320]{2,1,0:T(8,128)S(1)} %copy-done.3, f32[8,16,320]{2,1,0:T(8,128)S(1)} %copy-done.4, s32[1,1024]{1,0:T(1,128)S(1)} %bitcast.3, s32[1,640]{1,0:T(1,128)S(1)} %reshape.21.ws_ref, s32[1,640]{1,0:T(1,128)S(1)} %reshape.22.cnt_ref, ...), custom_call_target="tpu_custom_call" | custom-call | tf_op jit(solution)/shard_map/pallas_call | solution.py:382
  78.8 0.6 copy.14
  79.4 0.7 copy.15
  (1 shorter events, 0.0 us)
Async XLA Ops:
  3.3 1.7 %copy-start = (bf16[4,640,512]{2,1,0:T(8,128)(2,1)S(1)}, bf16[4,640,512]{2,1,0:T(8,128)(2,1)}, u32[]{:S(2)}) copy-start(bf16[4,640,512]{2,1,0:T(8,128)(2,1)} %constant.65.clone.hi_hbm) | copy-start | bytes 7864324
  5.0 1.1 %copy-start.1 = (bf16[576,512]{1,0:T(8,128)(2,1)S(1)}, bf16[576,512]{1,0:T(8,128)(2,1)}, u32[]{:S(2)}) copy-start(bf16[576,512]{1,0:T(8,128)(2,1)} %constant.67.clone.e_hbm) | copy-start | bytes 1769476
  6.1 1.0 %copy-start.2 = (bf16[512,512]{1,0:T(8,128)(2,1)S(1)}, bf16[512,512]{1,0:T(8,128)(2,1)}, u32[]{:S(2)}) copy-start(bf16[512,512]{1,0:T(8,128)(2,1)} %constant.68.clone.pi_hbm) | copy-start | bytes 1572868
  7.1 0.9 %copy-start.3 = (f32[8,16,320]{2,1,0:T(8,128)S(1)}, f32[8,16,320]{2,1,0:T(8,128)}, u32[]{:S(2)}) copy-start(f32[8,16,320]{2,1,0:T(8,128)} %u_ref.1) | copy-start | bytes 491524
  8.0 0.9 %copy-start.4 = (f32[8,16,320]{2,1,0:T(8,128)S(1)}, f32[8,16,320]{2,1,0:T(8,128)}, u32[]{:S(2)}) copy-start(f32[8,16,320]{2,1,0:T(8,128)} %v_ref.1) | copy-start | bytes 491524
  9.0 0.7 copy-start.5

commit v2 on v1

--- a/solution.py
+++ b/solution.py
@@ -73,6 +73,12 @@
 
 
 @functools.cache
+def order_table(waves):
+    lanes = wave_lanes(waves).reshape(1024)
+    return (np.arange(waves)[:, None] == lanes[None, :]).astype(ml_dtypes.bfloat16)
+
+
+@functools.cache
 def spread_table(cap):
     e = np.zeros((NZ, ROWS, 4, 128), np.float32)
     for z in range(NZ):
@@ -98,9 +104,9 @@
 
 
 def kernel(
-    u_ref, v_ref, tgt_ref, ws_ref, cnt_ref, visc_ref, basis_hbm, hi_hbm, lo_hbm, e_hbm, pi_hbm,
+    u_hbm, v_hbm, ws_hbm, cnt_hbm, visc_hbm, basis_hbm, hi_hbm, lo_hbm, e_hbm, pi_hbm, order_hbm,
     spec_ref, tend_ref,
-    basis, hi, lo, e_tab, pi_tab, onehot, damp,
+    u_ref, v_ref, ws_ref, cnt_ref, visc_ref, order, basis, hi, lo, e_tab, pi_tab, onehot, damp,
     send_l, recv_l, send_a, recv_a, send_b, recv_b, turned,
     back_t, send_b2, recv_b2, send_a2, recv_a2, send_l2, recv_l2,
     load_sem, sl, rl, sa, ra, sb, rb, sb2, rb2, sa2, ra2, sl2, rl2,
@@ -112,45 +118,52 @@
     core = lat % NC
     group = x * NC + core
     cap, degrees, half_lat = basis.shape
-    waves = ws_ref.shape[1]
+    waves = ws_ref.shape[0]
     sector = u_ref.shape[2]
 
     def in_group(g):
-        return ((g // NC) * (NZ * NC) + z * NC + g % NC, lon)
+        return (g // NC * (NZ * NC) + z * NC + g % NC, lon)
 
     def in_column(zz):
-        return (x * (NZ * NC) + zz * NC + core, lon)
+        return (lat + (zz - z) * NC, lon)
 
     def in_sector(s):
         return (lat, s)
 
-    barrier = pltpu.get_barrier_semaphore()
-
-    def greet(device_of, me, n):
-        def one(d, carry):
-            pl.semaphore_signal(barrier, inc=1, device_id=device_of((me + d) % n), device_id_type=MESH)
-            return carry
-
-        lax.fori_loop(1, n, one, 0)
-
-    greet(in_sector, lon, SECTORS)
-    greet(in_group, group, GROUPS)
-    greet(in_column, z, NZ)
+    def partners(me, n):
+        for d in sorted(range(1, n), key=lambda d: -min(d, n - d)):
+            to = me + d
+            yield jnp.where(to >= n, to - n, to)
 
     loads = [
         pltpu.make_async_copy(src, dst, load_sem.at[i])
         for i, (src, dst) in enumerate(
-            ((hi_hbm, hi), (lo_hbm, lo), (e_hbm, e_tab), (pi_hbm, pi_tab), (basis_hbm, basis))
+            (
+                (u_hbm, u_ref), (v_hbm, v_ref), (ws_hbm, ws_ref), (cnt_hbm, cnt_ref), (visc_hbm, visc_ref),
+                (order_hbm, order), (hi_hbm, hi), (lo_hbm, lo), (e_hbm, e_tab), (pi_hbm, pi_tab), (basis_hbm, basis),
+            )
         )
     ]
     for load in loads:
         load.start()
 
+    barrier = pltpu.get_barrier_semaphore()
+
+    def greet(device_of, me, n):
+        for to in partners(me, n):
+            pl.semaphore_signal(barrier, inc=1, device_id=device_of(to), device_id_type=MESH)
+
+    greet(in_sector, lon, SECTORS)
+    greet(in_group, group, GROUPS)
+    greet(in_column, z, NZ)
+
+    loads[0].wait()
+    loads[1].wait()
+
     def products(level, carry):
         u = u_ref[level]
         v = v_ref[level]
-        send_l[level, 0] = u * v
-        send_l[level, 1] = u * u - v * v
+        send_l[level] = jnp.concatenate([u * v, u * u - v * v], axis=1)
         return carry
 
     lax.fori_loop(0, SECTORS, products, 0)
@@ -158,49 +171,51 @@
     pl.semaphore_wait(barrier, SECTORS + GROUPS + NZ - 3)
 
     def exchange(src, dst, send_sem, recv_sem, device_of, me, n):
-        def copy(d):
-            to = (me + d) % n
-            return pltpu.make_async_remote_copy(
-                src_ref=src.at[to],
-                dst_ref=dst.at[me],
-                send_sem=send_sem.at[d],
-                recv_sem=recv_sem.at[d],
-                device_id=device_of(to),
-                device_id_type=MESH,
-            )
-
         def start():
-            def one(d, carry):
-                copy(d).start()
-                return carry
-
-            lax.fori_loop(1, n, one, 0)
-
-        def wait():
-            def one(d, carry):
-                copy(d).wait()
-                return carry
-
-            lax.fori_loop(1, n, one, 0)
-
-        return start, wait
-
-    start, wait = exchange(send_l, recv_l, sl, rl, in_sector, lon, SECTORS)
-    start()
-
-    target = tgt_ref[...]
+            for to in partners(me, n):
+                pltpu.make_async_remote_copy(
+                    src_ref=src.at[to],
+                    dst_ref=dst.at[me],
+                    send_sem=send_sem,
+                    recv_sem=recv_sem,
+                    device_id=device_of(to),
+                    device_id_type=MESH,
+                ).start()
+
+        def landed():
+            whole = dst.at[pl.ds(0, n - 1)]
+            pltpu.make_async_copy(whole, whole, recv_sem).wait()
+
+        def left():
+            whole = src.at[pl.ds(0, n - 1)]
+            pltpu.make_async_copy(whole, whole, send_sem).wait()
+
+        return start, landed, left
+
+    start, wait, left1 = exchange(send_l, recv_l, sl, rl, in_sector, lon, SECTORS)
+    start()
+
+    for load in loads[2:6]:
+        load.wait()
+    ws = ws_ref[...].reshape(1, waves)
+    owner = ws // cap
+    lane = (owner // (NZ * NC) * NC + owner % NC) * 128 + owner // NC % NZ * cap + ws % cap
+    digit = lax.broadcasted_iota(jnp.int32, (16, waves), 0)
+    digits = jnp.where(digit == 0, lane // 32, jnp.where(digit == 1, lane % 32, 1)).astype(F32)
+    ordered = nn(digits.astype(BF16), order[...])
+    target = (ordered[0:1] * 32.0 + ordered[1:2] + ordered[2:3] - 1.0).astype(jnp.int32)
     for b in range(GROUPS):
         ids = lax.broadcasted_iota(jnp.int32, (128, 1024), 0) + b * 128
         onehot[pl.ds(b * 128, 128), :] = jnp.where(ids == target, 1.0, 0.0).astype(BF16)
 
     rows40 = damp.shape[0]
     slot = lax.broadcasted_iota(jnp.int32, (rows40, waves), 0) // 4
-    here = (ws_ref[...] == lat * cap + slot) & (slot < cap)
+    here = (ws == lat * cap + slot) & (slot < cap)
     wave_ids = lax.broadcasted_iota(jnp.int32, (rows40, waves), 1)
     wave_here = jnp.sum(jnp.where(here, wave_ids, 0).astype(F32), axis=1, keepdims=True)
-    kept_here = jnp.sum(jnp.where(here, cnt_ref[...], 0).astype(F32), axis=1, keepdims=True)
+    kept_here = jnp.sum(jnp.where(here, cnt_ref[...].reshape(1, waves), 0).astype(F32), axis=1, keepdims=True)
     levels = lax.broadcasted_iota(jnp.int32, (1, SECTORS), 1)
-    rate = jnp.sum(jnp.where(levels == lon, visc_ref[...], 0.0), axis=1, keepdims=True)
+    rate = jnp.sum(jnp.where(levels == lon, visc_ref[...].reshape(1, SECTORS), 0.0), axis=1, keepdims=True)
     degree = lax.broadcasted_iota(jnp.int32, (rows40, degrees), 1).astype(F32)
     total = wave_here + degree
     q = total * (total + 1.0) / float(degrees * (degrees + 1))
@@ -208,27 +223,28 @@
     damp[...] = jnp.where(degree < kept_here, damping, 0.0)
 
     wait()
-    loads[0].wait()
-    loads[1].wait()
-
-    sums = []
-    for f in range(2):
-        a = [recv_l[s, f] for s in range(SECTORS)]
-        e0, e1, e2, e3 = (a[i] + a[i + 4] for i in range(4))
-        o0, o1, o2, o3 = (a[i] - a[i + 4] for i in range(4))
-        od = HALF * (o1 - o3)
-        os = HALF * (o1 + o3)
-        sums.append(
-            (
-                (e0 + e1 + e2 + e3, e0 - e1 + e2 - e3),
-                (o0 + od, -(os + o2)),
-                (e0 - e2, e3 - e1),
-                (o0 - od, o2 - os),
-            )
-        )
+    loads[6].wait()
+    loads[7].wait()
+
+    a = [recv_l[s] for s in range(SECTORS)]
+    e0, e1, e2, e3 = (a[i] + a[i + 4] for i in range(4))
+    o0, o1, o2, o3 = (a[i] - a[i + 4] for i in range(4))
+    od = HALF * (o1 - o3)
+    os = HALF * (o1 + o3)
+    sums = (
+        (e0 + e1 + e2 + e3, e0 - e1 + e2 - e3),
+        (o0 + od, -(os + o2)),
+        (e0 - e2, e3 - e1),
+        (o0 - od, o2 - os),
+    )
     for j in range(4):
+        one, two = sums[j]
         both = jnp.concatenate(
-            [jnp.concatenate([sums[f][j][0], sums[f][j][1]], axis=1) for f in range(2)], axis=0
+            [
+                jnp.concatenate([one[:, :sector], two[:, :sector]], axis=1),
+                jnp.concatenate([one[:, sector:], two[:, sector:]], axis=1),
+            ],
+            axis=0,
         )
         high = both.astype(BF16)
         low = (both - high.astype(F32)).astype(BF16)
@@ -241,18 +257,18 @@
     for g in range(GROUPS):
         for b in range(4):
             send_a[g, :, pl.ds(b * 128, 128)] = placed[b * 16 : b * 16 + 16, g * 128 : g * 128 + 128]
-    start, wait = exchange(send_a, recv_a, sa, ra, in_group, group, GROUPS)
+    start, wait, left2 = exchange(send_a, recv_a, sa, ra, in_group, group, GROUPS)
     start()
     recv_a[group] = send_a[group]
-    loads[2].wait()
+    loads[8].wait()
     wait()
     spread = nt(e_tab[...], recv_a[...].reshape(GROUPS * 16, 512)).astype(BF16)
     send_b[...] = spread.reshape(NZ, ROWS, 128)
-    start, wait = exchange(send_b, recv_b, sb, rb, in_column, z, NZ)
+    start, wait, left3 = exchange(send_b, recv_b, sb, rb, in_column, z, NZ)
     start()
     recv_b[z] = send_b[z]
-    loads[3].wait()
-    loads[4].wait()
+    loads[9].wait()
+    loads[10].wait()
     wait()
 
     quarters = NZ // 4
@@ -307,13 +323,13 @@
     mixed = nt(back_t[...].astype(BF16), pi_tab[...]).astype(BF16)
     for zz in range(NZ):
         send_b2[zz] = mixed[zz // 4 * ROWS : zz // 4 * ROWS + ROWS, zz % 4 * 128 : zz % 4 * 128 + 128]
-    start, wait = exchange(send_b2, recv_b2, sb2, rb2, in_column, z, NZ)
+    start, wait, left4 = exchange(send_b2, recv_b2, sb2, rb2, in_column, z, NZ)
     start()
     recv_b2[z] = send_b2[z]
     wait()
     joined = tn(recv_b2[...].reshape(NZ * ROWS, 128), e_tab[...]).astype(BF16)
     send_a2[...] = joined.reshape(GROUPS, 16, 512)
-    start, wait = exchange(send_a2, recv_a2, sa2, ra2, in_group, group, GROUPS)
+    start, wait, left5 = exchange(send_a2, recv_a2, sa2, ra2, in_group, group, GROUPS)
     start()
     recv_a2[group] = send_a2[group]
     wait()
@@ -350,34 +366,26 @@
         odd + ud + vs + v2,
     )
     for s in range(SECTORS):
-        send_l2[s] = grid[s].astype(BF16)
-    start, wait = exchange(send_l2, recv_l2, sl2, rl2, in_sector, lon, SECTORS)
+        send_l2[s] = jnp.concatenate([grid[s][:16], grid[s][16:]], axis=1).astype(BF16)
+    start, wait, left6 = exchange(send_l2, recv_l2, sl2, rl2, in_sector, lon, SECTORS)
     start()
     recv_l2[lon] = send_l2[lon]
     wait()
     for s in range(SECTORS):
-        tend_ref[s] = recv_l2[s].astype(F32).reshape(2, 16, sector)
+        both = recv_l2[s].astype(F32)
+        tend_ref[s, 0] = both[:, :sector]
+        tend_ref[s, 1] = both[:, sector:]
+    for left in (left1, left2, left3, left4, left5, left6):
+        left()
 
 
 def body(wind_u, wind_v, basis, wave_slots, degree_count, viscosity):
     levels, lat_rows, sector = wind_u.shape
     cap, degrees, half_lat = basis.shape
     waves = wave_slots.shape[0]
-    per = waves // SECTORS
     high, low = dft_table(sector * SECTORS, waves)
-    owner = wave_slots // cap
-    lane = (owner // (NZ * NC) * NC + owner % NC) * 128 + owner // NC % NZ * cap + wave_slots % cap
-    by_residue = lane.reshape(per, SECTORS).T
-    fill = jnp.full((256 - 2 * per,), -1, jnp.int32)
-    target = jnp.concatenate(
-        [
-            part
-            for j in range(4)
-            for part in (by_residue[j], by_residue[4 if j == 0 else SECTORS - j], fill)
-        ]
-    ).reshape(1, 1024)
     vmem = pl.BlockSpec(memory_space=pltpu.VMEM)
-    hbm = pl.BlockSpec(memory_space=pl.ANY)
+    hbm = pl.BlockSpec(memory_space=pltpu.HBM)
     dma = pltpu.SemaphoreType.DMA
     return pl.pallas_call(
         kernel,
@@ -385,9 +393,15 @@
             jax.ShapeDtypeStruct((cap, 1, 2, 2, degrees), F32),
             jax.ShapeDtypeStruct((levels, 2, lat_rows, sector), F32),
         ),
-        in_specs=[vmem] * 6 + [hbm] * 5,
+        in_specs=[hbm] * 11,
         out_specs=(vmem, vmem),
         scratch_shapes=[
+            pltpu.VMEM(wind_u.shape, F32),
+            pltpu.VMEM(wind_v.shape, F32),
+            pltpu.VMEM((waves,), jnp.int32),
+            pltpu.VMEM((waves,), jnp.int32),
+            pltpu.VMEM((levels,), F32),
+            pltpu.VMEM((waves, 1024), BF16),
             pltpu.VMEM(basis.shape, BF16),
             pltpu.VMEM(high.shape, BF16),
             pltpu.VMEM(low.shape, BF16),
@@ -395,8 +409,8 @@
             pltpu.VMEM((512, 512), BF16),
             pltpu.VMEM((1024, 1024), BF16),
             pltpu.VMEM((40, degrees), F32),
-            pltpu.VMEM((SECTORS, 2, lat_rows, sector), F32),
-            pltpu.VMEM((SECTORS, 2, lat_rows, sector), F32),
+            pltpu.VMEM((SECTORS, lat_rows, 2 * sector), F32),
+            pltpu.VMEM((SECTORS, lat_rows, 2 * sector), F32),
             pltpu.VMEM((GROUPS, 16, 512), BF16),
             pltpu.VMEM((GROUPS, 16, 512), BF16),
             pltpu.VMEM((NZ, ROWS, 128), BF16),
@@ -407,26 +421,31 @@
             pltpu.VMEM((NZ, ROWS, 128), BF16),
             pltpu.VMEM((GROUPS, 16, 512), BF16),
             pltpu.VMEM((GROUPS, 16, 512), BF16),
-            pltpu.VMEM((SECTORS, 2 * lat_rows, sector), BF16),
-            pltpu.VMEM((SECTORS, 2 * lat_rows, sector), BF16),
-            dma((5,)),
+            pltpu.VMEM((SECTORS, lat_rows, 2 * sector), BF16),
+            pltpu.VMEM((SECTORS, lat_rows, 2 * sector), BF16),
+            dma((11,)),
         ]
-        + [dma((n,)) for n in (8, 8, 8, 8, 12, 12, 12, 12, 8, 8, 8, 8)],
+        + [dma(())] * 12,
         compiler_params=pltpu.CompilerParams(
-            collective_id=0, has_side_effects=True, vmem_limit_bytes=48 * 2**20
+            collective_id=0, has_side_effects=True, vmem_limit_bytes=40 * 2**20
         ),
     )(
-        wind_u,
-        wind_v,
-        target,
-        wave_slots.reshape(1, waves),
-        degree_count.reshape(1, waves),
-        viscosity.reshape(1, levels),
-        basis,
-        jnp.asarray(high),
-        jnp.asarray(low),
-        jnp.asarray(spread_table(cap)),
-        jnp.asarray(lane_table()),
+        *(
+            pltpu.with_memory_space_constraint(operand, pltpu.HBM)
+            for operand in (
+                wind_u,
+                wind_v,
+                wave_slots,
+                degree_count,
+                viscosity,
+                basis,
+                jnp.asarray(high),
+                jnp.asarray(low),
+                jnp.asarray(spread_table(cap)),
+                jnp.asarray(lane_table()),
+                jnp.asarray(order_table(waves)),
+            )
+        )
     )
 
 

time: 81.1 us -> 68.1 us (0.84)
  local copies, waits for them, and re-layouts: 9.63 us -> 1.39 us
  Pallas kernels: 69.2 us -> 66 us
    unnamed x14 -> x2, local copies, waits for them, and re-layouts: 7.74 us -> 1.39 us
    pallas_call x1, Pallas kernels: 69.2 us -> 66 us  [body(): pl.pallas_call(kernel, out_shape=(jax.ShapeDtypeStruct((cap, 1, 2, 2, deg...]
    reshape x3 -> x0, local copies, waits for them, and re-layouts: 1.46 us -> none  [the longest x1 0.69 us: body(): degree_count.reshape(1, waves)]
where the time goes in v2:
time: 68.1 us; the launch traced here: 68 us
  Pallas kernels  66 us (97%)
  local copies, waits for them, and re-layouts  1.39 us (2%)
    pallas_call x1, Pallas kernels, body(): pl.pallas_call(kernel, out_shape=(jax.ShapeDtypeStruct((cap, 1, 2, 2, deg...  66 us
    unnamed x2, local copies, waits for them, and re-layouts  1.39 us

profile of v2, /device:TPU:1, one launch (start us, length us, event | category | flops | bytes accessed | tf_op | source)
XLA Modules:
  0.0 68.0 jit_solution(13908095554160575742)
XLA Ops:
  0.6 66.0 %shard_map.122 = (f32[9,1,2,2,640]{4,3,2,1,0:T(2,128)S(1)}, f32[8,2,16,320]{3,2,1,0:T(8,128)S(1)}) custom-call(f32[8,16,320]{2,1,0:T(8,128)} %u_hbm.1, f32[8,16,320]{2,1,0:T(8,128)} %v_hbm.1, s32[640]{0:T(1024)} %ws_hbm.1, s32[640]{0:T(1024)} %cnt_hbm.1, f32[8]{0:T(128)} %visc_hbm.1, bf16[9,640,768]{2,1,0:T(8,128)(2,1)} %basis_hbm.1, ...), custom_call_target="tpu_custom_call" | custom-call | tf_op jit(solution)/shard_map/pallas_call | solution.py:390
  66.6 0.6 copy.15
  67.2 0.7 %copy.16 = f32[8,2,16,320]{3,2,1,0:T(8,128)} copy(f32[8,2,16,320]{3,2,1,0:T(8,128)S(1)} %get-tuple-element.5) | data formatting | bytes 655360

commit v3 on v2

--- a/solution.py
+++ b/solution.py
@@ -17,7 +17,8 @@
 NX, NZ, NC = 4, 12, 2
 GROUPS = NX * NC
 SECTORS = 8
-ROWS = 48
+PARTS = 3
+ROWS = 16
 HALF = math.sqrt(0.5)
 
 
@@ -80,13 +81,13 @@
 
 @functools.cache
 def spread_table(cap):
-    e = np.zeros((NZ, ROWS, 4, 128), np.float32)
+    e = np.zeros((PARTS, NZ, ROWS, 4, 128), np.float32)
     for z in range(NZ):
         for k in range(cap):
             for f in range(2):
                 for r in range(2):
-                    e[z, k * 4 + f * 2 + r, r * 2 + f, z * cap + k] = 1.0
-    return e.reshape(NZ * ROWS, 512).astype(ml_dtypes.bfloat16)
+                    e[k // 4, z, k % 4 * 4 + f * 2 + r, r * 2 + f, z * cap + k] = 1.0
+    return e.reshape(PARTS * NZ * ROWS, 512).astype(ml_dtypes.bfloat16)
 
 
 @functools.cache
@@ -144,7 +145,7 @@
             )
         )
     ]
-    for load in loads:
+    for load in loads[:2]:
         load.start()
 
     barrier = pltpu.get_barrier_semaphore()
@@ -157,22 +158,18 @@
     greet(in_group, group, GROUPS)
     greet(in_column, z, NZ)
 
+    for load in loads[2:]:
+        load.start()
     loads[0].wait()
     loads[1].wait()
 
-    def products(level, carry):
-        u = u_ref[level]
-        v = v_ref[level]
-        send_l[level] = jnp.concatenate([u * v, u * u - v * v], axis=1)
-        return carry
-
-    lax.fori_loop(0, SECTORS, products, 0)
-    recv_l[lon] = send_l[lon]
     pl.semaphore_wait(barrier, SECTORS + GROUPS + NZ - 3)
 
     def exchange(src, dst, send_sem, recv_sem, device_of, me, n):
-        def start():
+        def start(prepare=None):
             for to in partners(me, n):
+                if prepare is not None:
+                    prepare(to)
                 pltpu.make_async_remote_copy(
                     src_ref=src.at[to],
                     dst_ref=dst.at[me],
@@ -192,8 +189,17 @@
 
         return start, landed, left
 
+    def products(level):
+        u = u_ref[level]
+        v = v_ref[level]
+        return jnp.concatenate([u * v, u * u - v * v], axis=1)
+
+    def prepare(level):
+        send_l[level] = products(level)
+
     start, wait, left1 = exchange(send_l, recv_l, sl, rl, in_sector, lon, SECTORS)
-    start()
+    start(prepare)
+    recv_l[lon] = products(lon)
 
     for load in loads[2:6]:
         load.wait()
@@ -263,72 +269,84 @@
     loads[8].wait()
     wait()
     spread = nt(e_tab[...], recv_a[...].reshape(GROUPS * 16, 512)).astype(BF16)
-    send_b[...] = spread.reshape(NZ, ROWS, 128)
-    start, wait, left3 = exchange(send_b, recv_b, sb, rb, in_column, z, NZ)
-    start()
-    recv_b[z] = send_b[z]
+    send_b[...] = spread.reshape(PARTS, NZ, ROWS, 128)
+    there = [
+        exchange(send_b.at[p], recv_b.at[p], sb.at[p], rb.at[p], in_column, z, NZ) for p in range(PARTS)
+    ]
+    back = [
+        exchange(send_b2.at[p], recv_b2.at[p], sb2.at[p], rb2.at[p], in_column, z, NZ)
+        for p in range(PARTS)
+    ]
+    for p in range(PARTS):
+        there[p][0]()
+    for p in range(PARTS):
+        recv_b[p, z] = send_b[p, z]
     loads[9].wait()
     loads[10].wait()
-    wait()
 
     quarters = NZ // 4
-    gathered = jnp.concatenate(
-        [
-            jnp.concatenate([recv_b[4 * i + k] for k in range(4)], axis=1)
-            for i in range(quarters)
-        ],
-        axis=0,
-    )
-    natural = nn(gathered, pi_tab[...])
     parity = jnp.where(lax.broadcasted_iota(jnp.int32, (8, degrees), 1) % 2 == 0, 1.0, -1.0)
     first = lax.broadcasted_iota(jnp.int32, (8, 1), 0) < 4
     blocks = half_lat // 128
-    for i in range((cap + 1) // 2):
-        r0 = 8 * i
-        north, south = [], []
-        for b in range(blocks):
-            xx, gg = b // quarters, b % quarters
-            north.append(natural[gg * ROWS + r0 : gg * ROWS + r0 + 8, xx * 128 : xx * 128 + 128])
-            xx, gg = NX - 1 - xx, quarters - 1 - gg
-            south.append(natural[gg * ROWS + r0 : gg * ROWS + r0 + 8, xx * 128 : xx * 128 + 128])
-        both = jnp.concatenate(
-            [jnp.concatenate(north, axis=1), jnp.concatenate(south, axis=1)], axis=0
-        ).astype(BF16)
-        raws = []
-        for k in (2 * i, 2 * i + 1):
-            if k < cap:
-                out = nt(both, basis[k])
-                raws.append(out[:8] + parity * out[8:])
-        raw = jnp.where(first, raws[0], raws[1] if len(raws) > 1 else 0.0)
-        spectral = raw * damp[pl.ds(r0, 8), :]
-        for k in (2 * i, 2 * i + 1):
-            if k < cap:
-                at = 4 * (k - 2 * i)
-                for f in range(2):
-                    spec_ref[k, 0, f] = spectral[at + 2 * f : at + 2 * f + 2]
-        rounded = spectral.astype(BF16).astype(F32)
-        pair = jnp.concatenate([rounded, rounded * parity], axis=0).astype(BF16)
-        outs = [nn(pair, basis[k]) for k in (2 * i, 2 * i + 1) if k < cap]
-        keep = jnp.concatenate([first, first], axis=0)
-        back = jnp.where(keep, outs[0], outs[1] if len(outs) > 1 else 0.0)
-        back = back * (1.0 / math.sqrt(degrees))
-        for b in range(blocks):
-            xx, gg = b // quarters, b % quarters
-            back_t[pl.ds(gg * ROWS + r0, 8), pl.ds(xx * 128, 128)] = back[:8, b * 128 : b * 128 + 128]
-            xx, gg = NX - 1 - xx, quarters - 1 - gg
-            back_t[pl.ds(gg * ROWS + r0, 8), pl.ds(xx * 128, 128)] = back[8:, b * 128 : b * 128 + 128]
-    for gg in range(quarters):
-        back_t[pl.ds(gg * ROWS + 40, 8), :] = jnp.zeros((8, 512), F32)
-
-    mixed = nt(back_t[...].astype(BF16), pi_tab[...]).astype(BF16)
-    for zz in range(NZ):
-        send_b2[zz] = mixed[zz // 4 * ROWS : zz // 4 * ROWS + ROWS, zz % 4 * 128 : zz % 4 * 128 + 128]
-    start, wait, left4 = exchange(send_b2, recv_b2, sb2, rb2, in_column, z, NZ)
-    start()
-    recv_b2[z] = send_b2[z]
-    wait()
-    joined = tn(recv_b2[...].reshape(NZ * ROWS, 128), e_tab[...]).astype(BF16)
-    send_a2[...] = joined.reshape(GROUPS, 16, 512)
+    for p in range(PARTS):
+        there[p][1]()
+        gathered = jnp.concatenate(
+            [
+                jnp.concatenate([recv_b[p, 4 * i + k] for k in range(4)], axis=1)
+                for i in range(quarters)
+            ],
+            axis=0,
+        )
+        natural = nn(gathered, pi_tab[...])
+        for i in range(2 * p, min(2 * p + 2, (cap + 1) // 2)):
+            r0 = 8 * (i - 2 * p)
+            north, south = [], []
+            for b in range(blocks):
+                xx, gg = b // quarters, b % quarters
+                north.append(natural[gg * ROWS + r0 : gg * ROWS + r0 + 8, xx * 128 : xx * 128 + 128])
+                xx, gg = NX - 1 - xx, quarters - 1 - gg
+                south.append(natural[gg * ROWS + r0 : gg * ROWS + r0 + 8, xx * 128 : xx * 128 + 128])
+            both = jnp.concatenate(
+                [jnp.concatenate(north, axis=1), jnp.concatenate(south, axis=1)], axis=0
+            ).astype(BF16)
+            raws = []
+            for k in (2 * i, 2 * i + 1):
+                if k < cap:
+                    out = nt(both, basis[k])
+                    raws.append(out[:8] + parity * out[8:])
+            raw = jnp.where(first, raws[0], raws[1] if len(raws) > 1 else 0.0)
+            spectral = raw * damp[pl.ds(8 * i, 8), :]
+            for k in (2 * i, 2 * i + 1):
+                if k < cap:
+                    at = 4 * (k - 2 * i)
+                    for f in range(2):
+                        spec_ref[k, 0, f] = spectral[at + 2 * f : at + 2 * f + 2]
+            rounded = spectral.astype(BF16).astype(F32)
+            pair = jnp.concatenate([rounded, rounded * parity], axis=0).astype(BF16)
+            outs = [nn(pair, basis[k]) for k in (2 * i, 2 * i + 1) if k < cap]
+            keep = jnp.concatenate([first, first], axis=0)
+            synth = jnp.where(keep, outs[0], outs[1] if len(outs) > 1 else 0.0)
+            synth = synth * (1.0 / math.sqrt(degrees))
+            for b in range(blocks):
+                xx, gg = b // quarters, b % quarters
+                back_t[p, pl.ds(gg * ROWS + r0, 8), pl.ds(xx * 128, 128)] = synth[:8, b * 128 : b * 128 + 128]
+                xx, gg = NX - 1 - xx, quarters - 1 - gg
+                back_t[p, pl.ds(gg * ROWS + r0, 8), pl.ds(xx * 128, 128)] = synth[8:, b * 128 : b * 128 + 128]
+        for gg in range(quarters):
+            if 2 * p + 2 > (cap + 1) // 2:
+                back_t[p, pl.ds(gg * ROWS + 8, 8), :] = jnp.zeros((8, 512), F32)
+        mixed = nt(back_t[p].astype(BF16), pi_tab[...]).astype(BF16)
+        for zz in range(NZ):
+            send_b2[p, zz] = mixed[zz // 4 * ROWS : zz // 4 * ROWS + ROWS, zz % 4 * 128 : zz % 4 * 128 + 128]
+        back[p][0]()
+        recv_b2[p, z] = send_b2[p, z]
+
+    joined = 0.0
+    for p in range(PARTS):
+        back[p][1]()
+        rows = NZ * ROWS
+        joined += tn(recv_b2[p].reshape(rows, 128), e_tab[pl.ds(p * rows, rows), :])
+    send_a2[...] = joined.astype(BF16).reshape(GROUPS, 16, 512)
     start, wait, left5 = exchange(send_a2, recv_a2, sa2, ra2, in_group, group, GROUPS)
     start()
     recv_a2[group] = send_a2[group]
@@ -375,7 +393,7 @@
         both = recv_l2[s].astype(F32)
         tend_ref[s, 0] = both[:, :sector]
         tend_ref[s, 1] = both[:, sector:]
-    for left in (left1, left2, left3, left4, left5, left6):
+    for left in (left1, left2, left5, left6, *(e[2] for e in there), *(e[2] for e in back)):
         left()
 
 
@@ -405,7 +423,7 @@
             pltpu.VMEM(basis.shape, BF16),
             pltpu.VMEM(high.shape, BF16),
             pltpu.VMEM(low.shape, BF16),
-            pltpu.VMEM((NZ * ROWS, 512), BF16),
+            pltpu.VMEM((PARTS * NZ * ROWS, 512), BF16),
             pltpu.VMEM((512, 512), BF16),
             pltpu.VMEM((1024, 1024), BF16),
             pltpu.VMEM((40, degrees), F32),
@@ -413,19 +431,19 @@
             pltpu.VMEM((SECTORS, lat_rows, 2 * sector), F32),
             pltpu.VMEM((GROUPS, 16, 512), BF16),
             pltpu.VMEM((GROUPS, 16, 512), BF16),
-            pltpu.VMEM((NZ, ROWS, 128), BF16),
-            pltpu.VMEM((NZ, ROWS, 128), BF16),
+            pltpu.VMEM((PARTS, NZ, ROWS, 128), BF16),
+            pltpu.VMEM((PARTS, NZ, ROWS, 128), BF16),
             pltpu.VMEM((64, 1024), BF16),
-            pltpu.VMEM((NZ // 4 * ROWS, 512), F32),
-            pltpu.VMEM((NZ, ROWS, 128), BF16),
-            pltpu.VMEM((NZ, ROWS, 128), BF16),
+            pltpu.VMEM((PARTS, NZ // 4 * ROWS, 512), F32),
+            pltpu.VMEM((PARTS, NZ, ROWS, 128), BF16),
+            pltpu.VMEM((PARTS, NZ, ROWS, 128), BF16),
             pltpu.VMEM((GROUPS, 16, 512), BF16),
             pltpu.VMEM((GROUPS, 16, 512), BF16),
             pltpu.VMEM((SECTORS, lat_rows, 2 * sector), BF16),
             pltpu.VMEM((SECTORS, lat_rows, 2 * sector), BF16),
             dma((11,)),
         ]
-        + [dma(())] * 12,
+        + [dma(())] * 4 + [dma((PARTS,))] * 4 + [dma(())] * 4,
         compiler_params=pltpu.CompilerParams(
             collective_id=0, has_side_effects=True, vmem_limit_bytes=40 * 2**20
         ),

time: 68.1 us -> 66.2 us (0.972)
  Pallas kernels: 66 us -> 64.1 us
    pallas_call x1, Pallas kernels: 66 us -> 64.1 us  [body(): pl.pallas_call(kernel, out_shape=(jax.ShapeDtypeStruct((cap, 1, 2, 2, deg...]
where the time goes in v3:
time: 66.2 us; the launch traced here: 66.1 us
  Pallas kernels  64.1 us (97%)
  local copies, waits for them, and re-layouts  1.39 us (2%)
    pallas_call x1, Pallas kernels, body(): pl.pallas_call(kernel, out_shape=(jax.ShapeDtypeStruct((cap, 1, 2, 2, deg...  64.1 us
    unnamed x2, local copies, waits for them, and re-layouts  1.39 us

profile of v3, /device:TPU:1, one launch (start us, length us, event | category | flops | bytes accessed | tf_op | source)
XLA Modules:
  0.0 66.1 jit_solution(458999727180111915)
XLA Ops:
  0.6 64.1 %shard_map.122 = (f32[9,1,2,2,640]{4,3,2,1,0:T(2,128)S(1)}, f32[8,2,16,320]{3,2,1,0:T(8,128)S(1)}) custom-call(f32[8,16,320]{2,1,0:T(8,128)} %u_hbm.1, f32[8,16,320]{2,1,0:T(8,128)} %v_hbm.1, s32[640]{0:T(1024)} %ws_hbm.1, s32[640]{0:T(1024)} %cnt_hbm.1, f32[8]{0:T(128)} %visc_hbm.1, bf16[9,640,768]{2,1,0:T(8,128)(2,1)} %basis_hbm.1, ...), custom_call_target="tpu_custom_call" | custom-call | tf_op jit(solution)/shard_map/pallas_call | solution.py:408
  64.7 0.6 copy.15
  65.3 0.7 %copy.16 = f32[8,2,16,320]{3,2,1,0:T(8,128)} copy(f32[8,2,16,320]{3,2,1,0:T(8,128)S(1)} %get-tuple-element.5) | data formatting | bytes 655360

commit v4 on v3

--- a/solution.py
+++ b/solution.py
@@ -17,8 +17,9 @@
 NX, NZ, NC = 4, 12, 2
 GROUPS = NX * NC
 SECTORS = 8
-PARTS = 3
+PARTS = 2
 ROWS = 16
+REST = 4
 HALF = math.sqrt(0.5)
 
 
@@ -82,12 +83,15 @@
 @functools.cache
 def spread_table(cap):
     e = np.zeros((PARTS, NZ, ROWS, 4, 128), np.float32)
+    rest = np.zeros((NZ, REST, 4, 128), np.float32)
     for z in range(NZ):
         for k in range(cap):
             for f in range(2):
                 for r in range(2):
-                    e[k // 4, z, k % 4 * 4 + f * 2 + r, r * 2 + f, z * cap + k] = 1.0
-    return e.reshape(PARTS * NZ * ROWS, 512).astype(ml_dtypes.bfloat16)
+                    rows = e[k // 4] if k < 4 * PARTS else rest
+                    rows[z, k % 4 * 4 + f * 2 + r, r * 2 + f, z * cap + k] = 1.0
+    both = np.concatenate([e.reshape(PARTS * NZ * ROWS, 512), rest.reshape(NZ * REST, 512)])
+    return both.astype(ml_dtypes.bfloat16)
 
 
 @functools.cache
@@ -109,7 +113,7 @@
     spec_ref, tend_ref,
     u_ref, v_ref, ws_ref, cnt_ref, visc_ref, order, basis, hi, lo, e_tab, pi_tab, onehot, damp,
     send_l, recv_l, send_a, recv_a, send_b, recv_b, turned,
-    back_t, send_b2, recv_b2, send_a2, recv_a2, send_l2, recv_l2,
+    back_t, send_b2, recv_b2, send_c, recv_c, send_c2, recv_c2, send_a2, recv_a2, send_l2, recv_l2,
     load_sem, sl, rl, sa, ra, sb, rb, sb2, rb2, sa2, ra2, sl2, rl2,
 ):
     lat = lax.axis_index("lat")
@@ -268,19 +272,26 @@
     recv_a[group] = send_a[group]
     loads[8].wait()
     wait()
-    spread = nt(e_tab[...], recv_a[...].reshape(GROUPS * 16, 512)).astype(BF16)
-    send_b[...] = spread.reshape(PARTS, NZ, ROWS, 128)
-    there = [
-        exchange(send_b.at[p], recv_b.at[p], sb.at[p], rb.at[p], in_column, z, NZ) for p in range(PARTS)
-    ]
-    back = [
-        exchange(send_b2.at[p], recv_b2.at[p], sb2.at[p], rb2.at[p], in_column, z, NZ)
-        for p in range(PARTS)
-    ]
-    for p in range(PARTS):
+    spread = nt(e_tab[...], recv_a[...].reshape(GROUPS * 16, 512))
+    full = PARTS * NZ * ROWS
+    send_b[...] = spread[:full].astype(BF16).reshape(PARTS, NZ, ROWS, 128)
+    for zz in range(NZ):
+        send_c[zz] = spread[full + REST * zz : full + REST * zz + REST]
+
+    def over_z(src, dst, send_sems, recv_sems, rest_src, rest_dst):
+        pieces = [(src.at[p], dst.at[p]) for p in range(PARTS)] + [(rest_src, rest_dst)]
+        return [
+            exchange(a, b, send_sems.at[p], recv_sems.at[p], in_column, z, NZ)
+            for p, (a, b) in enumerate(pieces)
+        ]
+
+    there = over_z(send_b, recv_b, sb, rb, send_c, recv_c)
+    back = over_z(send_b2, recv_b2, sb2, rb2, send_c2, recv_c2)
+    for p in range(PARTS + 1):
         there[p][0]()
     for p in range(PARTS):
         recv_b[p, z] = send_b[p, z]
+    recv_c[z] = send_c[z]
     loads[9].wait()
     loads[10].wait()
 
@@ -288,15 +299,17 @@
     parity = jnp.where(lax.broadcasted_iota(jnp.int32, (8, degrees), 1) % 2 == 0, 1.0, -1.0)
     first = lax.broadcasted_iota(jnp.int32, (8, 1), 0) < 4
     blocks = half_lat // 128
-    for p in range(PARTS):
+    pad = jnp.zeros((ROWS - REST, 512), F32)
+    for p in range(PARTS + 1):
         there[p][1]()
-        gathered = jnp.concatenate(
-            [
-                jnp.concatenate([recv_b[p, 4 * i + k] for k in range(4)], axis=1)
-                for i in range(quarters)
-            ],
-            axis=0,
-        )
+        gathered = []
+        for i in range(quarters):
+            if p < PARTS:
+                gathered.append(jnp.concatenate([recv_b[p, 4 * i + k] for k in range(4)], axis=1))
+            else:
+                rest = jnp.concatenate([recv_c[4 * i + k] for k in range(4)], axis=1)
+                gathered.append(jnp.concatenate([rest, pad], axis=0).astype(BF16))
+        gathered = jnp.concatenate(gathered, axis=0)
         natural = nn(gathered, pi_tab[...])
         for i in range(2 * p, min(2 * p + 2, (cap + 1) // 2)):
             r0 = 8 * (i - 2 * p)
@@ -335,17 +348,27 @@
         for gg in range(quarters):
             if 2 * p + 2 > (cap + 1) // 2:
                 back_t[p, pl.ds(gg * ROWS + 8, 8), :] = jnp.zeros((8, 512), F32)
-        mixed = nt(back_t[p].astype(BF16), pi_tab[...]).astype(BF16)
+        mixed = nt(back_t[p].astype(BF16), pi_tab[...])
         for zz in range(NZ):
-            send_b2[p, zz] = mixed[zz // 4 * ROWS : zz // 4 * ROWS + ROWS, zz % 4 * 128 : zz % 4 * 128 + 128]
+            piece = mixed[zz // 4 * ROWS : zz // 4 * ROWS + ROWS, zz % 4 * 128 : zz % 4 * 128 + 128]
+            if p < PARTS:
+                send_b2[p, zz] = piece.astype(BF16)
+            else:
+                send_c2[zz] = piece[:REST]
         back[p][0]()
-        recv_b2[p, z] = send_b2[p, z]
+        if p < PARTS:
+            recv_b2[p, z] = send_b2[p, z]
+        else:
+            recv_c2[z] = send_c2[z]
 
     joined = 0.0
     for p in range(PARTS):
         back[p][1]()
         rows = NZ * ROWS
         joined += tn(recv_b2[p].reshape(rows, 128), e_tab[pl.ds(p * rows, rows), :])
+    back[PARTS][1]()
+    rest = jnp.concatenate([recv_c2[zz] for zz in range(NZ)], axis=0).astype(BF16)
+    joined += tn(rest, e_tab[pl.ds(full, NZ * REST), :])
     send_a2[...] = joined.astype(BF16).reshape(GROUPS, 16, 512)
     start, wait, left5 = exchange(send_a2, recv_a2, sa2, ra2, in_group, group, GROUPS)
     start()
@@ -423,7 +446,7 @@
             pltpu.VMEM(basis.shape, BF16),
             pltpu.VMEM(high.shape, BF16),
             pltpu.VMEM(low.shape, BF16),
-            pltpu.VMEM((PARTS * NZ * ROWS, 512), BF16),
+            pltpu.VMEM((PARTS * NZ * ROWS + NZ * REST, 512), BF16),
             pltpu.VMEM((512, 512), BF16),
             pltpu.VMEM((1024, 1024), BF16),
             pltpu.VMEM((40, degrees), F32),
@@ -434,16 +457,20 @@
             pltpu.VMEM((PARTS, NZ, ROWS, 128), BF16),
             pltpu.VMEM((PARTS, NZ, ROWS, 128), BF16),
             pltpu.VMEM((64, 1024), BF16),
-            pltpu.VMEM((PARTS, NZ // 4 * ROWS, 512), F32),
+            pltpu.VMEM((PARTS + 1, NZ // 4 * ROWS, 512), F32),
             pltpu.VMEM((PARTS, NZ, ROWS, 128), BF16),
             pltpu.VMEM((PARTS, NZ, ROWS, 128), BF16),
+            pltpu.VMEM((NZ, REST, 128), F32),
+            pltpu.VMEM((NZ, REST, 128), F32),
+            pltpu.VMEM((NZ, REST, 128), F32),
+            pltpu.VMEM((NZ, REST, 128), F32),
             pltpu.VMEM((GROUPS, 16, 512), BF16),
             pltpu.VMEM((GROUPS, 16, 512), BF16),
             pltpu.VMEM((SECTORS, lat_rows, 2 * sector), BF16),
             pltpu.VMEM((SECTORS, lat_rows, 2 * sector), BF16),
             dma((11,)),
         ]
-        + [dma(())] * 4 + [dma((PARTS,))] * 4 + [dma(())] * 4,
+        + [dma(())] * 4 + [dma((PARTS + 1,))] * 4 + [dma(())] * 4,
         compiler_params=pltpu.CompilerParams(
             collective_id=0, has_side_effects=True, vmem_limit_bytes=40 * 2**20
         ),

time: 66.2 us -> 65.9 us (level)
  no operation moved by 1% of the time
where the time goes in v4:
time: 65.9 us; the launch traced here: 65.8 us
  Pallas kernels  63.7 us (97%)
  local copies, waits for them, and re-layouts  1.39 us (2%)
    pallas_call x1, Pallas kernels, body(): pl.pallas_call(kernel, out_shape=(jax.ShapeDtypeStruct((cap, 1, 2, 2, deg...  63.7 us
    unnamed x2, local copies, waits for them, and re-layouts  1.39 us

profile of v4, /device:TPU:1, one launch (start us, length us, event | category | flops | bytes accessed | tf_op | source)
XLA Modules:
  0.0 65.8 jit_solution(3735026782555657836)
XLA Ops:
  0.6 63.7 %shard_map.122 = (f32[9,1,2,2,640]{4,3,2,1,0:T(2,128)S(1)}, f32[8,2,16,320]{3,2,1,0:T(8,128)S(1)}) custom-call(f32[8,16,320]{2,1,0:T(8,128)} %u_hbm.1, f32[8,16,320]{2,1,0:T(8,128)} %v_hbm.1, s32[640]{0:T(1024)} %ws_hbm.1, s32[640]{0:T(1024)} %cnt_hbm.1, f32[8]{0:T(128)} %visc_hbm.1, bf16[9,640,768]{2,1,0:T(8,128)(2,1)} %basis_hbm.1, ...), custom_call_target="tpu_custom_call" | custom-call | tf_op jit(solution)/shard_map/pallas_call | solution.py:431
  64.4 0.6 copy.15
  65.0 0.7 %copy.16 = f32[8,2,16,320]{3,2,1,0:T(8,128)} copy(f32[8,2,16,320]{3,2,1,0:T(8,128)S(1)} %get-tuple-element.5) | data formatting | bytes 655360

commit v5 on v4

--- a/solution.py
+++ b/solution.py
@@ -109,9 +109,9 @@
 
 
 def kernel(
-    u_hbm, v_hbm, ws_hbm, cnt_hbm, visc_hbm, basis_hbm, hi_hbm, lo_hbm, e_hbm, pi_hbm, order_hbm,
+    u_hbm, v_hbm, ws_hbm, cnt_hbm, visc_hbm, basis_hbm, hi_hbm, lo_hbm, e_hbm, pi_hbm, order_hbm, hi_t_hbm, pi_t_hbm,
     spec_ref, tend_ref,
-    u_ref, v_ref, ws_ref, cnt_ref, visc_ref, order, basis, hi, lo, e_tab, pi_tab, onehot, damp,
+    u_ref, v_ref, ws_ref, cnt_ref, visc_ref, order, basis, hi, lo, e_tab, pi_tab, hi_t, pi_t, onehot, damp,
     send_l, recv_l, send_a, recv_a, send_b, recv_b, turned,
     back_t, send_b2, recv_b2, send_c, recv_c, send_c2, recv_c2, send_a2, recv_a2, send_l2, recv_l2,
     load_sem, sl, rl, sa, ra, sb, rb, sb2, rb2, sa2, ra2, sl2, rl2,
@@ -146,6 +146,7 @@
             (
                 (u_hbm, u_ref), (v_hbm, v_ref), (ws_hbm, ws_ref), (cnt_hbm, cnt_ref), (visc_hbm, visc_ref),
                 (order_hbm, order), (hi_hbm, hi), (lo_hbm, lo), (e_hbm, e_tab), (pi_hbm, pi_tab), (basis_hbm, basis),
+                (pi_t_hbm, pi_t), (hi_t_hbm, hi_t),
             )
         )
     ]
@@ -292,8 +293,8 @@
     for p in range(PARTS):
         recv_b[p, z] = send_b[p, z]
     recv_c[z] = send_c[z]
-    loads[9].wait()
-    loads[10].wait()
+    for load in loads[9:]:
+        load.wait()
 
     quarters = NZ // 4
     parity = jnp.where(lax.broadcasted_iota(jnp.int32, (8, degrees), 1) % 2 == 0, 1.0, -1.0)
@@ -348,7 +349,7 @@
         for gg in range(quarters):
             if 2 * p + 2 > (cap + 1) // 2:
                 back_t[p, pl.ds(gg * ROWS + 8, 8), :] = jnp.zeros((8, 512), F32)
-        mixed = nt(back_t[p].astype(BF16), pi_tab[...])
+        mixed = nn(back_t[p].astype(BF16), pi_t[...])
         for zz in range(NZ):
             piece = mixed[zz // 4 * ROWS : zz // 4 * ROWS + ROWS, zz % 4 * 128 : zz % 4 * 128 + 128]
             if p < PARTS:
@@ -390,7 +391,7 @@
         lhs = jnp.concatenate(
             [waved[:32, j * 256 : j * 256 + 256], waved[32:, j * 256 : j * 256 + 256]], axis=1
         )
-        out = nt(lhs, hi[j]) + nt(lhs, lo[j])
+        out = nn(lhs, hi_t[j])
         parts.append((out[:, :sector], out[:, sector:]))
     (u0, u4), (u1, v1), (u2, v2), (u3, v3) = parts
     even, odd = u0 + u4, u0 - u4
@@ -434,7 +435,7 @@
             jax.ShapeDtypeStruct((cap, 1, 2, 2, degrees), F32),
             jax.ShapeDtypeStruct((levels, 2, lat_rows, sector), F32),
         ),
-        in_specs=[hbm] * 11,
+        in_specs=[hbm] * 13,
         out_specs=(vmem, vmem),
         scratch_shapes=[
             pltpu.VMEM(wind_u.shape, F32),
@@ -447,6 +448,8 @@
             pltpu.VMEM(high.shape, BF16),
             pltpu.VMEM(low.shape, BF16),
             pltpu.VMEM((PARTS * NZ * ROWS + NZ * REST, 512), BF16),
+            pltpu.VMEM((512, 512), BF16),
+            pltpu.VMEM((high.shape[0], high.shape[2], high.shape[1]), BF16),
             pltpu.VMEM((512, 512), BF16),
             pltpu.VMEM((1024, 1024), BF16),
             pltpu.VMEM((40, degrees), F32),
@@ -468,7 +471,7 @@
             pltpu.VMEM((GROUPS, 16, 512), BF16),
             pltpu.VMEM((SECTORS, lat_rows, 2 * sector), BF16),
             pltpu.VMEM((SECTORS, lat_rows, 2 * sector), BF16),
-            dma((11,)),
+            dma((13,)),
         ]
         + [dma(())] * 4 + [dma((PARTS + 1,))] * 4 + [dma(())] * 4,
         compiler_params=pltpu.CompilerParams(
@@ -489,6 +492,8 @@
                 jnp.asarray(spread_table(cap)),
                 jnp.asarray(lane_table()),
                 jnp.asarray(order_table(waves)),
+                jnp.asarray(np.ascontiguousarray(high.transpose(0, 2, 1))),
+                jnp.asarray(np.ascontiguousarray(lane_table().T)),
             )
         )
     )

time: 65.9 us -> 64.7 us (0.982)
  Pallas kernels: 63.7 us -> 62.6 us
    pallas_call x1, Pallas kernels: 63.7 us -> 62.6 us  [body(): pl.pallas_call(kernel, out_shape=(jax.ShapeDtypeStruct((cap, 1, 2, 2, deg...]
where the time goes in v5:
time: 64.7 us; the launch traced here: 64.6 us
  Pallas kernels  62.6 us (97%)
  local copies, waits for them, and re-layouts  1.39 us (2%)
    pallas_call x1, Pallas kernels, body(): pl.pallas_call(kernel, out_shape=(jax.ShapeDtypeStruct((cap, 1, 2, 2, deg...  62.6 us
    unnamed x2, local copies, waits for them, and re-layouts  1.39 us

profile of v5, /device:TPU:1, one launch (start us, length us, event | category | flops | bytes accessed | tf_op | source)
XLA Modules:
  0.0 64.6 jit_solution(5443876420837864045)
XLA Ops:
  0.6 62.6 %shard_map.140 = (f32[9,1,2,2,640]{4,3,2,1,0:T(2,128)S(1)}, f32[8,2,16,320]{3,2,1,0:T(8,128)S(1)}) custom-call(f32[8,16,320]{2,1,0:T(8,128)} %u_hbm.1, f32[8,16,320]{2,1,0:T(8,128)} %v_hbm.1, s32[640]{0:T(1024)} %ws_hbm.1, s32[640]{0:T(1024)} %cnt_hbm.1, f32[8]{0:T(128)} %visc_hbm.1, bf16[9,640,768]{2,1,0:T(8,128)(2,1)} %basis_hbm.1, ...), custom_call_target="tpu_custom_call" | custom-call | tf_op jit(solution)/shard_map/pallas_call | solution.py:432
  63.2 0.6 copy.17
  63.9 0.7 %copy.18 = f32[8,2,16,320]{3,2,1,0:T(8,128)} copy(f32[8,2,16,320]{3,2,1,0:T(8,128)S(1)} %get-tuple-element.5) | data formatting | bytes 655360

commit v6 on v5

--- a/solution.py
+++ b/solution.py
@@ -273,11 +273,8 @@
     recv_a[group] = send_a[group]
     loads[8].wait()
     wait()
-    spread = nt(e_tab[...], recv_a[...].reshape(GROUPS * 16, 512))
+    arrived = recv_a[...].reshape(GROUPS * 16, 512)
     full = PARTS * NZ * ROWS
-    send_b[...] = spread[:full].astype(BF16).reshape(PARTS, NZ, ROWS, 128)
-    for zz in range(NZ):
-        send_c[zz] = spread[full + REST * zz : full + REST * zz + REST]
 
     def over_z(src, dst, send_sems, recv_sems, rest_src, rest_dst):
         pieces = [(src.at[p], dst.at[p]) for p in range(PARTS)] + [(rest_src, rest_dst)]
@@ -288,8 +285,14 @@
 
     there = over_z(send_b, recv_b, sb, rb, send_c, recv_c)
     back = over_z(send_b2, recv_b2, sb2, rb2, send_c2, recv_c2)
-    for p in range(PARTS + 1):
+    for p in range(PARTS):
+        spread = nt(e_tab[pl.ds(p * NZ * ROWS, NZ * ROWS), :], arrived)
+        send_b[p] = spread.astype(BF16).reshape(NZ, ROWS, 128)
         there[p][0]()
+    spread = nt(e_tab[pl.ds(full, NZ * REST), :], arrived)
+    for zz in range(NZ):
+        send_c[zz] = spread[REST * zz : REST * zz + REST]
+    there[PARTS][0]()
     for p in range(PARTS):
         recv_b[p, z] = send_b[p, z]
     recv_c[z] = send_c[z]

time: 64.7 us -> 64.2 us (level)
  no operation moved by 1% of the time
where the time goes in v6:
time: 64.2 us; the launch traced here: 64.1 us
  Pallas kernels  62.1 us (97%)
  local copies, waits for them, and re-layouts  1.39 us (2%)
    pallas_call x1, Pallas kernels, body(): pl.pallas_call(kernel, out_shape=(jax.ShapeDtypeStruct((cap, 1, 2, 2, deg...  62.1 us
    unnamed x2, local copies, waits for them, and re-layouts  1.39 us

profile of v6, /device:TPU:1, one launch (start us, length us, event | category | flops | bytes accessed | tf_op | source)
XLA Modules:
  0.0 64.1 jit_solution(10180339784183293905)
XLA Ops:
  0.6 62.1 %shard_map.140 = (f32[9,1,2,2,640]{4,3,2,1,0:T(2,128)S(1)}, f32[8,2,16,320]{3,2,1,0:T(8,128)S(1)}) custom-call(f32[8,16,320]{2,1,0:T(8,128)} %u_hbm.1, f32[8,16,320]{2,1,0:T(8,128)} %v_hbm.1, s32[640]{0:T(1024)} %ws_hbm.1, s32[640]{0:T(1024)} %cnt_hbm.1, f32[8]{0:T(128)} %visc_hbm.1, bf16[9,640,768]{2,1,0:T(8,128)(2,1)} %basis_hbm.1, ...), custom_call_target="tpu_custom_call" | custom-call | tf_op jit(solution)/shard_map/pallas_call | solution.py:435
  62.7 0.6 %copy.17 = f32[9,1,2,2,640]{4,3,2,1,0:T(2,128)} copy(f32[9,1,2,2,640]{4,3,2,1,0:T(2,128)S(1)} %get-tuple-element.4) | data formatting | bytes 184320
  63.3 0.7 %copy.18 = f32[8,2,16,320]{3,2,1,0:T(8,128)} copy(f32[8,2,16,320]{3,2,1,0:T(8,128)S(1)} %get-tuple-element.5) | data formatting | bytes 655360
